TPU v7x, 512 devices: a whole 4x4x16 slice. The times are simulated.
512 devices in a mesh: dp: 32 (over z, y_hi), mp: 16 (over y_lo, x, core).
Axes of the slice: x: 4, y: 4 (y_hi: 2, y_lo: 2; y = y_hi * 2 + y_lo), z: 16, core: 2. Of those that a mesh axis runs over, the one named last changes fastest.
Arguments:
- activations: bfloat16 [16384, 4096], P('dp', 'mp'), may hold values from -6 to 6
- out_grads: bfloat16 [16384, 4096], P('dp', 'mp'), may hold values from -6 to 6
- valid_len: int32 [32], P('dp'), may hold values from 1 to 512, 12288 in all
- basis_act: bfloat16 [4096, 4096], P('dp', 'mp'), may hold values from -0.09375 to 0.09375
- basis_grad: bfloat16 [4096, 4096], P('dp', 'mp'), may hold values from -0.09375 to 0.09375
- eig_state: float32 [32, 2, 4096], P('dp', None, 'mp'), may hold values from 0.05 to 2
- owner_table: int32 [2], replicated, may hold values from 0 to 31, as said below
Outputs:
- precond_update: bfloat16 [4096, 4096], P(None, 'mp')
- new_state: float32 [32, 2, 4096], P('dp', None, 'mp')
Inputs may be any that keep to these rules, and one draw needn't show every extreme that they name: `valid_len`: some shard has all 512 tokens valid. `owner_table`: the two owners are different ranks, and one of them is rank 32 - 1.
All inputs are finite; a program needn't handle non-finite values.
Results may differ from a plain program's by a relative error of at most 0.03.
Values may be sent and summed in bfloat16 or wider, within the bound.
No kernel may reach another device: no remote copies, remote signals or barrier semaphores. Data moves between devices by JAX's collectives and lax.ppermute only.
A program may use at most 64 MiB of HBM per device.

v0:
```python
import math

import jax
import jax.numpy as jnp
from jax import lax
from jax.sharding import PartitionSpec as P

EMA_WEIGHT = 0.5
DAMPING = 0.01


def from_root(array, axis, root):
    mine = lax.axis_index(axis) == root
    return lax.psum(jnp.where(mine, array, jnp.zeros_like(array)), axis)


def owner_row(values, source):
    return from_root(values, "dp", source)


def local(activations, out_grads, valid_len, basis_act, basis_grad, eig_state, owner_table):
    tokens_dev = activations.shape[0]
    token_total = tokens_dev * lax.axis_size("dp")
    full_act, full_grad = (
        lax.all_gather(activations, "mp", axis=1, tiled=True),
        lax.all_gather(out_grads, "mp", axis=1, tiled=True),
    )
    next_act = jnp.dot(
        full_act,
        lax.all_gather(basis_act, "dp", axis=0, tiled=True),
        preferred_element_type=jnp.float32,
    )
    next_grad = jnp.dot(
        full_grad,
        lax.all_gather(basis_grad, "dp", axis=0, tiled=True),
        preferred_element_type=jnp.float32,
    )
    proj_act = next_act
    proj_grad = next_grad
    proj_act = proj_act.astype(jnp.bfloat16)
    proj_grad = proj_grad.astype(jnp.bfloat16)
    valid_mask = (lax.iota(jnp.int32, tokens_dev) < valid_len[0]).astype(jnp.float32)
    wide_act = proj_act.astype(jnp.float32)
    wide_grad = proj_grad.astype(jnp.float32)
    part_stat_act = jnp.sum(valid_mask[:, None] * (wide_act * wide_act), axis=0) / token_total
    part_stat_grad = jnp.sum(valid_mask[:, None] * (wide_grad * wide_grad), axis=0) / token_total
    stat_act, stat_grad = lax.psum((part_stat_act, part_stat_grad), "dp")
    state_act = owner_row(eig_state[0, 0], owner_table[0])
    state_grad = owner_row(eig_state[0, 1], owner_table[1])
    eigen_act = EMA_WEIGHT * state_act + (1.0 - EMA_WEIGHT) * stat_act
    eigen_grad = EMA_WEIGHT * state_grad + (1.0 - EMA_WEIGHT) * stat_grad
    new_state = jnp.stack([eigen_act, eigen_grad])[None]
    grad_rows_all = lax.all_gather(eigen_grad, "mp", axis=0, tiled=True)
    masked_act = jnp.where(valid_mask[:, None] > 0, proj_act, jnp.zeros_like(proj_act))
    partial_term = lax.dot_general(
        lax.all_gather(proj_grad, "mp", axis=1, tiled=True),
        masked_act,
        (((0,), (0,)), ((), ())),
        preferred_element_type=jnp.float32,
    )
    scale_root = math.sqrt(token_total)
    summed = lax.psum(partial_term.astype(jnp.bfloat16), "dp").astype(jnp.float32)
    denom = grad_rows_all[:, None] * eigen_act[None, :] + DAMPING
    precond_update = (summed / scale_root / denom).astype(jnp.bfloat16)
    return (precond_update, new_state)


def solution(mesh):
    placed = (
        P("dp", "mp"),
        P("dp", "mp"),
        P("dp"),
        P("dp", "mp"),
        P("dp", "mp"),
        P("dp", None, "mp"),
        P(),
    )
    return jax.shard_map(
        local,
        mesh=mesh,
        in_specs=placed,
        out_specs=(P(None, "mp"), P("dp", None, "mp")),
        check_vma=False,
    )
```

profile of v0, /device:TPU:2, one launch (start us, length us, event | category | flops | bytes accessed | tf_op | source)
XLA Modules:
  0.0 805.8 jit_solution(732862429005116579)
XLA Ops:
  7.2 0.0 all-gather.15.cloned.1.call-start
  7.2 0.7 all-gather.15.cloned.1.call-update
  7.9 0.0 all-gather.13.cloned.1.call-start
  7.9 0.7 all-gather.13.cloned.1.call-update
  8.6 0.0 all-gather.9.cloned.1.call-start
  8.7 0.7 all-gather.9.cloned.1.call-update
  9.4 0.0 all-gather.7.cloned.1.call-start
  9.4 0.5 all-gather.7.cloned.1.call-update
  10.0 0.0 all-gather.11.cloned.1.call-start
  10.7 155.1 %all-gather.15.cloned.1.call-done = bf16[4096,256]{1,0:T(8,128)(2,1)} async-done(((bf16[128,256]{1,0:T(8,128)(2,1)}), bf16[4096,256]{1,0:T(8,128)(2,1)}) %all-gather.15.cloned.1.call-update) | async-done | bytes 2097168 | tf_op jit(solution)/shard_map/all_gather | solution.py:30
  165.8 49.0 %all-gather.13.cloned.1.call-done = bf16[512,4096]{1,0:T(8,128)(2,1)} async-done(((bf16[512,256]{1,0:T(8,128)(2,1)}), bf16[512,4096]{1,0:T(8,128)(2,1)}) %all-gather.13.cloned.1.call-update) | async-done | bytes 4194320 | tf_op jit(solution)/shard_map/all_gather | solution.py:25
  214.8 4.1 convolution_convert_fusion.1
  218.9 149.4 %all-gather.9.cloned.1.call-done = bf16[4096,256]{1,0:T(8,128)(2,1)} async-done(((bf16[128,256]{1,0:T(8,128)(2,1)}), bf16[4096,256]{1,0:T(8,128)(2,1)}) %all-gather.9.cloned.1.call-update) | async-done | bytes 2097168 | tf_op jit(solution)/shard_map/all_gather | solution.py:35
  368.4 48.9 %all-gather.7.cloned.1.call-done = bf16[512,4096]{1,0:T(8,128)(2,1)} async-done(((bf16[512,256]{1,0:T(8,128)(2,1)}), bf16[512,4096]{1,0:T(8,128)(2,1)}) %all-gather.7.cloned.1.call-update) | async-done | bytes 4194320 | tf_op jit(solution)/shard_map/all_gather | solution.py:26
  417.3 4.8 multiply_reduce_fusion.1
  422.1 0.0 all-reduce.3.cloned.1.call-start
  422.2 52.9 %all-gather.11.cloned.1.call-done = bf16[512,4096]{1,0:T(8,128)(2,1)} async-done(((bf16[512,256]{1,0:T(8,128)(2,1)}), bf16[512,4096]{1,0:T(8,128)(2,1)}) %all-gather.11.cloned.1.call-update) | async-done | bytes 4194320 | tf_op jit(solution)/shard_map/all_gather | solution.py:56
  475.2 4.9 convolution_convert_fusion
  480.1 0.6 fusion.5
  482.0 78.0 %all-reduce = (f32[256]{0:T(256)S(1)}, f32[256]{0:T(256)S(1)}) all-reduce(f32[256]{0:T(256)S(1)} %get-tuple-element.11, f32[256]{0:T(256)S(1)} %get-tuple-element.12), channel_id=1, replica_groups=mesh['dp'=32,'mp'=16] {'dp'}, use_global_device_ids=true, to_apply=%region_4.5 | all-reduce | flops 512 | bytes 4096 | tf_op jit(solution)/shard_map/psum | solution.py:14
  560.0 16.7 %all-gather = f32[16,1,256]{2,1,0:T(1,128)S(1)} all-gather(f32[1,1,256]{2,1,0:T(1,128)S(1)} %bitcast.20), channel_id=1, replica_groups=mesh['dp'=32,'mp'=16] {'mp'}, dimensions={0}, use_global_device_ids=true | all-gather | bytes 17408 | tf_op jit(solution)/shard_map/all_gather | solution.py:53
  576.7 0.6 maximum_bitcast_fusion
  577.3 218.4 %all-reduce.3.cloned.1.call-done = bf16[4096,256]{1,0:T(8,128)(2,1)} async-done(((bf16[4096,256]{1,0:T(8,128)(2,1)}), bf16[4096,256]{1,0:T(8,128)(2,1)}) %all-reduce.3.cloned.1.call-update) | async-done | bytes 2097168 | tf_op jit(solution)/shard_map/psum | solution.py:62
  795.7 3.2 divide_convert_fusion
  (12 shorter events, 0.1 us)
Async XLA Ops:
  7.2 158.6 %all-gather.15.cloned.1.call-start = ((), (), s32[]{:S(2)}) async-start(), calls=%async_computation.4 | async-start | bytes 2162688 | tf_op jit(solution)/shard_map/all_gather | solution.py:30
  7.9 206.9 %all-gather.13.cloned.1.call-start = ((), (), s32[]{:S(2)}) async-start(), calls=%async_computation.3 | async-start | bytes 4456448 | tf_op jit(solution)/shard_map/all_gather | solution.py:25
  8.6 359.7 %all-gather.9.cloned.1.call-start = ((), (), s32[]{:S(2)}) async-start(), calls=%async_computation.1 | async-start | bytes 2162688 | tf_op jit(solution)/shard_map/all_gather | solution.py:35
  9.4 407.9 %all-gather.7.cloned.1.call-start = ((), (), s32[]{:S(2)}) async-start(), calls=%async_computation | async-start | bytes 4456448 | tf_op jit(solution)/shard_map/all_gather | solution.py:26
  10.0 465.2 %all-gather.11.cloned.1.call-start = ((), (), s32[]{:S(2)}) async-start(), calls=%async_computation.2 | async-start | bytes 4456448 | tf_op jit(solution)/shard_map/all_gather | solution.py:56
  422.1 373.6 %all-reduce.3.cloned.1.call-start = ((), (), s32[]{:S(2)}) async-start(), calls=%async_computation.5 | async-start | bytes 4194304 | tf_op jit(solution)/shard_map/psum | solution.py:62
  422.2 57.9 %copy-start.1 = (s32[2]{0:T(128)S(1)}, s32[2]{0:T(128)}, u32[]{:S(2)}) copy-start(s32[2]{0:T(128)} %param.13) | copy-start | bytes 28
  422.2 59.8 %copy-start = (f32[1,2,256]{2,1,0:T(2,128)S(1)}, f32[1,2,256]{2,1,0:T(2,128)}, u32[]{:S(2)}) copy-start(f32[1,2,256]{2,1,0:T(2,128)} %param.12) | copy-start | bytes 6148
Sparse Core Ops, SparseCore 0:
  11.1 154.6 all-gather.14
  167.8 46.9 all-gather.12
  217.9 150.4 all-gather.8
  370.3 46.9 all-gather.6
  422.2 52.8 all-gather.10
  480.2 315.4 all-reduce.2
where the time goes:
time: 806 us
  waiting for transfers between devices  676 us (84%)
  blocking collectives  94.7 us (12%)
  between operations  16.1 us (2%)
  matrix products  13.8 us (2%)
    psum x1, waiting for transfers between devices, local(): lax.psum(partial_term.astype(jnp.bfloat16), 'dp').astype(jnp.float32)  218 us
    all_gather x1, waiting for transfers between devices, local(): lax.all_gather(basis_act, 'dp', axis=0, tiled=True)  155 us
    all_gather x1, waiting for transfers between devices, local(): lax.all_gather(basis_grad, 'dp', axis=0, tiled=True)  149 us
    psum x1, blocking collectives, from_root(): return lax.psum(jnp.where(mine, array, jnp.zeros_like(array)), axis)  78 us
    all_gather x1, waiting for transfers between devices, local(): lax.all_gather(proj_grad, 'mp', axis=1, tiled=True)  52.9 us
    all_gather x1, waiting for transfers between devices, local(): lax.all_gather(activations, 'mp', axis=1, tiled=True)  49 us
    all_gather x1, waiting for transfers between devices, local(): lax.all_gather(out_grads, 'mp', axis=1, tiled=True)  48.9 us
    all_gather x1, blocking collectives, local(): grad_rows_all = lax.all_gather(eigen_grad, 'mp', axis=0, tiled=True)  16.7 us
  transfers between devices with their start and end apart: 6, of which 6 were waited for; matrix products, arithmetic and copies ran while one was open for 1% of the time, Pallas kernels for 0%

commit v1 on v0

v1 whole, which is shorter than its diff:
```python
import functools
import math

import jax
import jax.numpy as jnp
from jax import lax
from jax.experimental import pallas as pl
from jax.experimental.pallas import tpu as pltpu
from jax.sharding import Mesh, PartitionSpec as P

EMA_WEIGHT = 0.5
DAMPING = 0.01
DP = ("z", "h")
MP = ("l", "x", "c")
BF16 = jnp.bfloat16
F32 = jnp.float32


def swap(array, axis):
    return lax.ppermute(array, axis, [(0, 1), (1, 0)])


def turn(array, axis, by):
    size = lax.axis_size(axis)
    return lax.ppermute(array, axis, [(i, (i + by) % size) for i in range(size)])


def project_kernel(scalars, own, other, basis, act_out, grad_out, stat_out, acc_act, acc_grad):
    step = pl.program_id(0)
    core = scalars[0]
    width = act_out.shape[1]

    @pl.when(step == 0)
    def _():
        acc_act[...] = jnp.zeros_like(acc_act)
        acc_grad[...] = jnp.zeros_like(acc_grad)

    def mul(a, b):
        return jnp.dot(a, b, preferred_element_type=F32)

    mine, theirs = basis[core], basis[1 - core]
    acc_act[...] += mul(own[0, 0], mine[:, :width]) + mul(other[0, 0], theirs[:, :width])
    acc_grad[...] += mul(own[0, 1], mine[:, width:]) + mul(other[0, 1], theirs[:, width:])

    @pl.when(step == pl.num_programs(0) - 1)
    def _():
        rows = lax.broadcasted_iota(jnp.int32, acc_act.shape, 0)
        valid = rows < scalars[1]
        act = jnp.where(valid, acc_act[...].astype(BF16).astype(F32), 0.0)
        grad = acc_grad[...].astype(BF16)
        wide = jnp.where(valid, grad.astype(F32), 0.0)
        act_out[...] = act.astype(BF16)
        grad_out[...] = grad
        stat_out[0:1] = jnp.sum(act * act, axis=0, keepdims=True)
        stat_out[1:2] = jnp.sum(wide * wide, axis=0, keepdims=True)


def project(scalars, own, other, basis):
    steps, _, tokens, depth = own.shape
    width = basis.shape[-1] // 2
    blocks = pl.BlockSpec((1, 2, tokens, depth), lambda k, s: (k, 0, 0, 0))
    return pl.pallas_call(
        project_kernel,
        grid_spec=pltpu.PrefetchScalarGridSpec(
            num_scalar_prefetch=1,
            grid=(steps,),
            in_specs=[blocks, blocks, pl.BlockSpec((2, depth, 2 * width), lambda k, s: (k, 0, 0))],
            out_specs=[
                pl.BlockSpec((tokens, width), lambda k, s: (0, 0)),
                pl.BlockSpec((tokens, width), lambda k, s: (0, 0)),
                pl.BlockSpec((2, width), lambda k, s: (0, 0)),
            ],
            scratch_shapes=[pltpu.VMEM((tokens, width), F32)] * 2,
        ),
        out_shape=[
            jax.ShapeDtypeStruct((tokens, width), BF16),
            jax.ShapeDtypeStruct((tokens, width), BF16),
            jax.ShapeDtypeStruct((2, width), F32),
        ],
        compiler_params=pltpu.CompilerParams(vmem_limit_bytes=32 << 20),
        cost_estimate=pl.CostEstimate(flops=4 * steps * 4 * tokens * depth * width, bytes_accessed=14 << 20, transcendentals=0),
    )(scalars, own, other, basis)


def term_kernel(scalars, *refs):
    grads, acts, out = refs[:4], refs[4:8], refs[8]
    parts, rows, width = out.shape[0] // 4, out.shape[2], out.shape[3]
    for g in range(4):
        block = scalars[g]
        for a in range(4):
            tile = lax.dot_general(grads[g][...], acts[a][...], (((0,), (0,)), ((), ())), preferred_element_type=F32)
            tile = tile.astype(BF16).reshape(parts, rows, width)
            for p in range(parts):
                out[block * parts + p, scalars[4 + a]] = tile[p]


def term(scalars, grads, acts, chunks):
    tokens, width = acts[0].shape
    rows = 4 * width // chunks
    whole = pl.BlockSpec(memory_space=pltpu.VMEM)
    return pl.pallas_call(
        term_kernel,
        in_specs=[pl.BlockSpec(memory_space=pltpu.SMEM)] + [whole] * 8,
        out_specs=whole,
        out_shape=jax.ShapeDtypeStruct((chunks, 4, rows, width), BF16),
        compiler_params=pltpu.CompilerParams(vmem_limit_bytes=32 << 20),
        cost_estimate=pl.CostEstimate(flops=32 * tokens * width * width, bytes_accessed=4 << 20, transcendentals=0),
    )(scalars, *grads, *acts)


def local(activations, out_grads, valid_len, basis_act, basis_grad, eig_state, owner_table):
    z, h, l, x, c = (lax.axis_index(a) for a in ("z", "h", "l", "x", "c"))
    chunks = lax.axis_size("z")
    tokens, width = activations.shape
    token_total = tokens * chunks * lax.axis_size("h")

    bases = jnp.concatenate([basis_act, basis_grad], axis=1)
    paired = swap(bases, "h")
    bases = jnp.concatenate([jnp.where(h == 0, bases, paired), jnp.where(h == 0, paired, bases)], axis=0)
    inputs = jnp.stack([activations, out_grads])
    bases, inputs = lax.optimization_barrier((bases, inputs))
    all_bases = lax.all_gather(bases, "z", axis=0)
    own = lax.all_to_all(jnp.broadcast_to(inputs[None], (8, *inputs.shape)), ("l", "x"), 0, 0)
    other = swap(own, "c")

    scalars = jnp.stack([c, valid_len[0]]).astype(jnp.int32)
    act, grad, stat = project(scalars, own, other, all_bases)

    acts = [act, turn(act, "x", 1), turn(act, "x", -1), turn(act, "x", 2)]
    far = swap(grad, "l")
    grads = [grad, far, swap(grad, "c"), swap(far, "c")]
    q = 2 * l + c
    places = jnp.stack([q, q ^ 2, q ^ 1, q ^ 3, x, (x - 1) % 4, (x + 1) % 4, (x + 2) % 4]).astype(jnp.int32)
    partial_term = term(places, grads, acts, chunks)
    summed = lax.psum_scatter(partial_term, "z", scatter_dimension=0, tiled=True)[0]

    rank = z * 2 + h
    mine = (owner_table == rank).astype(F32)
    part = (1.0 - EMA_WEIGHT) * (stat / token_total) + EMA_WEIGHT * mine[:, None] * eig_state[0]
    part = lax.psum(part, "z")
    eigen = part + swap(part, "h")
    new_state = eigen[None]
    eigen_rows = lax.all_gather(eigen[1], MP, axis=0).reshape(2, 4, 2, width)
    eigen_rows = lax.dynamic_index_in_dim(eigen_rows, z // 8, 0, keepdims=False)
    eigen_rows = lax.dynamic_index_in_dim(eigen_rows, (z // 4) % 2, 1, keepdims=False)
    rows = partial_term.shape[2]
    eigen_rows = lax.dynamic_slice_in_dim(eigen_rows, (z % 4) * rows, rows, axis=1)

    moved = lax.all_to_all(jnp.broadcast_to(summed[None], (2, *summed.shape)).reshape(8, rows, width), ("h", "x"), 0, 0)
    moved = moved.reshape(2, 4, rows, width).astype(F32)
    denom = eigen_rows[:, :, None] * eigen[0][None, None, :] + DAMPING
    values = (moved[0] + moved[1]) / math.sqrt(token_total) / denom

    top = jnp.max(jnp.abs(values))
    power = jnp.where(top > 0, jnp.clip(jnp.floor(14.0 - jnp.log2(top)), -100.0, 126.0), 0.0)
    sent = jnp.concatenate(
        [(values * jnp.exp2(power)).astype(jnp.float16).reshape(4 * rows, width), jnp.full((16, width), power, jnp.float16)],
        axis=0,
    )
    got = lax.all_gather(sent, "z", axis=0)
    back = jnp.exp2(-got[:, 4 * rows, 0].astype(F32))
    full = got[:, : 4 * rows].astype(F32) * back[:, None, None]
    full = full.astype(BF16).reshape(2, 2, 4, 4, rows, width).transpose(0, 3, 1, 2, 4, 5)
    return (full.reshape(chunks * 4 * rows, width), new_state)


def solution(mesh):
    fine = Mesh(mesh.devices.reshape(16, 2, 2, 4, 2), ("z", "h", "l", "x", "c"))
    placed = (P(DP, MP), P(DP, MP), P(DP), P(DP, MP), P(DP, MP), P(DP, None, MP), P())
    return jax.shard_map(
        local, mesh=fine, in_specs=placed, out_specs=(P(None, MP), P(DP, None, MP)), check_vma=False
    )
```

time: 806 us -> 300 us (0.37)
  the two profiles are of different devices: /device:TPU:2 before, /device:TPU:16 now
where the time goes in v1:
time: 300 us; the launch traced here: 299 us
  waiting for transfers between devices  122 us (41%)
  blocking collectives  92.3 us (31%)
  starting transfers between devices  42.5 us (14%)
  between operations  16.4 us (5%)
  Pallas kernels  11.3 us (4%)
  local copies, waits for them, and re-layouts  10.8 us (4%)
  other arithmetic  3.89 us (1%)
    all_to_all x1, waiting for transfers between devices, local(): lax.all_to_all(jnp.broadcast_to(inputs[None], (8, *inputs.shape)), ('l',...  46.4 us
    all_gather x1, blocking collectives, local(): got = lax.all_gather(sent, 'z', axis=0)  43.4 us
    reduce_scatter x1, waiting for transfers between devices, local(): lax.psum_scatter(partial_term, 'z', scatter_dimension=0, tiled=True)[0]  32 us
    psum x1, blocking collectives, local(): part = lax.psum(part, 'z')  29.7 us
    all_gather x1, waiting for transfers between devices, local(): all_bases = lax.all_gather(bases, 'z', axis=0)  28.7 us
    ppermute x6, starting transfers between devices, swap(): return lax.ppermute(array, axis, [(0, 1), (1, 0)])  19.9 us
    all_gather x1, blocking collectives, local(): eigen_rows = lax.all_gather(eigen[1], MP, axis=0).reshape(2, 4, 2, width)  19.3 us
    ppermute x6, waiting for transfers between devices, swap(): return lax.ppermute(array, axis, [(0, 1), (1, 0)])  12.8 us
  transfers between devices with their start and end apart: 13, of which 7 were waited for; matrix products, arithmetic and copies ran while one was open for 1% of the time, Pallas kernels for 0%

profile of v1, /device:TPU:16, one launch (start us, length us, event | category | flops | bytes accessed | tf_op | source)
XLA Modules:
  0.0 299.5 jit_solution(5582604115443059715)
XLA Ops:
  8.9 7.6 %collective-permute-start = (bf16[128,512]{1,0:T(8,128)(2,1)S(1)}, bf16[128,512]{1,0:T(8,128)(2,1)S(1)}, u32[]{:S(2)}, u32[]{:S(2)}) collective-permute-start(bf16[128,512]{1,0:T(8,128)(2,1)S(1)} %constant_dynamic-update-slice_fusion), channel_id=1, source_target_pairs={{0,16},{16,0},{1,17},{17,1},{2,18},{18,2},{3,19},{19,3},{4,20},{20... | collective-permute-start | bytes 393224 | tf_op jit(solution)/shard_map/ppermute | solution.py:20
  17.6 1.8 collective-permute-done
  20.1 2.4 broadcast_in_dim.8
  22.5 4.6 %all-to-all-start = ((bf16[8,2,512,256]{3,2,1,0:T(8,128)(2,1)}), bf16[8,2,512,256]{3,2,1,0:T(8,128)(2,1)}, u32[]{:S(2)}, u32[]{:S(2)}) async-start(bf16[8,2,512,256]{3,2,1,0:T(8,128)(2,1)} %broadcast_in_dim.8), calls=%async_computation | async-start | bytes 8388608 | tf_op jit(solution)/shard_map/all_to_all | solution.py:123
  27.9 46.4 %all-to-all-done.own = bf16[8,2,512,256]{3,2,1,0:T(8,128)(2,1)} async-done(((bf16[8,2,512,256]{3,2,1,0:T(8,128)(2,1)}), bf16[8,2,512,256]{3,2,1,0:T(8,128)(2,1)}, u32[]{:S(2)}, u32[]{:S(2)}) %all-to-all-start) | async-done | bytes 4194336 | tf_op jit(solution)/shard_map/all_to_all | solution.py:123
  74.3 1.9 collective-permute-start.1
  76.9 6.7 %collective-permute-done.1.other = bf16[8,2,512,256]{3,2,1,0:T(8,128)(2,1)} collective-permute-done((bf16[8,2,512,256]{3,2,1,0:T(8,128)(2,1)}, bf16[8,2,512,256]{3,2,1,0:T(8,128)(2,1)}, u32[]{:S(2)}, u32[]{:S(2)}) %collective-permute-start.1) | collective-permute-done | bytes 4194336 | tf_op jit(solution)/shard_map/ppermute | solution.py:20
  83.6 28.7 %all-gather.6.cloned.1.call-done = bf16[4096,512]{1,0:T(8,128)(2,1)} async-done(((bf16[256,512]{1,0:T(8,128)(2,1)}), bf16[4096,512]{1,0:T(8,128)(2,1)}) %all-gather.6.cloned.1.call-update) | async-done | bytes 4194320 | tf_op jit(solution)/shard_map/all_gather | solution.py:122
  112.3 2.2 copy-done
  114.5 8.1 %shard_map.86 = (bf16[512,256]{1,0:T(8,128)(2,1)S(1)}, bf16[512,256]{1,0:T(8,128)(2,1)S(1)}, f32[2,256]{1,0:T(2,128)S(1)}) custom-call(s32[2]{0:T(128)S(1)} %pad_add_fusion.scalars, bf16[8,2,512,256]{3,2,1,0:T(8,128)(2,1)} %all-to-all-done.own, bf16[8,2,512,256]{3,2,1,0:T(8,128)(2,1)} %collective-permute-done.1.other, bf16[16,256,512]{2,1,0:T(8,128)(2,1)S(1)} %bitcast.36), custom_call_target="tpu_custom_call" | custom-call | flops 4294967296 | bytes 14680064 | tf_op jit(solution)/shard_map/pallas_call | solution.py:62
  122.7 3.4 %collective-permute-start.2 = (bf16[512,256]{1,0:T(8,128)(2,1)S(1)}, bf16[512,256]{1,0:T(8,128)(2,1)S(1)}, u32[]{:S(2)}, u32[]{:S(2)}) collective-permute-start(bf16[512,256]{1,0:T(8,128)(2,1)S(1)} %get-tuple-element.9.refs_0_), channel_id=1, source_target_pairs={{0,8},{8,0},{1,9},{9,1},{2,10},{10,2},{3,11},{11,3},{4,12},{12,4},... | collective-permute-start | bytes 786440 | tf_op jit(solution)/shard_map/ppermute | solution.py:20
  126.1 3.2 %collective-permute-start.5 = (bf16[512,256]{1,0:T(8,128)(2,1)S(1)}, bf16[512,256]{1,0:T(8,128)(2,1)S(1)}, u32[]{:S(2)}, u32[]{:S(2)}) collective-permute-start(bf16[512,256]{1,0:T(8,128)(2,1)S(1)} %get-tuple-element.10.refs_4_), channel_id=1, source_target_pairs={{0,2},{2,4},{4,6},{6,0},{1,3},{3,5},{5,7},{7,1},{8,10},{10,12},{12... | collective-permute-start | bytes 786440 | tf_op jit(solution)/shard_map/ppermute | solution.py:25
  129.3 3.8 %collective-permute-start.6 = (bf16[512,256]{1,0:T(8,128)(2,1)S(1)}, bf16[512,256]{1,0:T(8,128)(2,1)S(1)}, u32[]{:S(2)}, u32[]{:S(2)}) collective-permute-start(bf16[512,256]{1,0:T(8,128)(2,1)S(1)} %get-tuple-element.10.refs_4_), channel_id=1, source_target_pairs={{0,6},{2,0},{4,2},{6,4},{1,7},{3,1},{5,3},{7,5},{8,14},{10,8},{12,... | collective-permute-start | bytes 786440 | tf_op jit(solution)/shard_map/ppermute | solution.py:25
  133.1 3.7 %collective-permute-start.7 = (bf16[512,256]{1,0:T(8,128)(2,1)S(1)}, bf16[512,256]{1,0:T(8,128)(2,1)S(1)}, u32[]{:S(2)}, u32[]{:S(2)}) collective-permute-start(bf16[512,256]{1,0:T(8,128)(2,1)S(1)} %get-tuple-element.10.refs_4_), channel_id=1, source_target_pairs={{0,4},{2,6},{4,0},{6,2},{1,5},{3,7},{5,1},{7,3},{8,12},{10,14},{12... | collective-permute-start | bytes 786440 | tf_op jit(solution)/shard_map/ppermute | solution.py:25
  136.8 1.9 collective-permute-start.3
  138.8 2.4 collective-permute-start.4
  142.9 3.2 %shard_map.87 = bf16[16,4,64,256]{3,2,1,0:T(8,128)(2,1)} custom-call(s32[8]{0:T(128)S(1)} %stack.50.scalars, bf16[512,256]{1,0:T(8,128)(2,1)S(1)} %get-tuple-element.9.refs_0_, bf16[512,256]{1,0:T(8,128)(2,1)S(1)} %collective-permute-done.2.refs_1_, bf16[512,256]{1,0:T(8,128)(2,1)S(1)} %collective-permute-done.3.refs_2_, ...), custom_call_target="tpu_custom_call" | custom-call | flops 1073741824 | bytes 4194304 | tf_op jit(solution)/shard_map/pallas_call | solution.py:101
  146.2 29.7 %psum.7 = f32[2,256]{1,0:T(2,128)S(1)} all-reduce(f32[2,256]{1,0:T(2,128)S(1)} %fusion.3), channel_id=1, replica_groups=mesh['z'=16,'h'=2,'l'=2,'x'=4,'c'=2] {'z'}, use_global_device_ids=true, to_apply=%region_1.2 | all-reduce | flops 512 | bytes 4096 | tf_op jit(solution)/shard_map/psum | solution.py:140
  175.9 2.7 collective-permute-start.8
  178.7 4.2 %collective-permute-done.8 = f32[2,256]{1,0:T(2,128)S(1)} collective-permute-done((f32[2,256]{1,0:T(2,128)S(1)}, f32[2,256]{1,0:T(2,128)S(1)}, u32[]{:S(2)}, u32[]{:S(2)}) %collective-permute-start.8) | collective-permute-done | bytes 2080 | tf_op jit(solution)/shard_map/ppermute | solution.py:20
  182.9 32.0 %reduce-scatter.2.cloned.1.call-done = bf16[1,4,64,256]{3,2,1,0:T(8,128)(2,1)} async-done(((bf16[16,4,64,256]{3,2,1,0:T(8,128)(2,1)}), bf16[1,4,64,256]{3,2,1,0:T(8,128)(2,1)}) %reduce-scatter.2.cloned.1.call-update) | async-done | bytes 131088 | tf_op jit(solution)/shard_map/reduce_scatter | solution.py:135
  216.5 7.2 %all-to-all-start.1 = ((bf16[8,64,256]{2,1,0:T(8,128)(2,1)}), bf16[8,64,256]{2,1,0:T(8,128)(2,1)S(1)}, u32[]{:S(2)}, u32[]{:S(2)}) async-start(bf16[8,64,256]{2,1,0:T(8,128)(2,1)} %bitcast.13), calls=%async_computation.2 | async-start | bytes 524288 | tf_op jit(solution)/shard_map/all_to_all | solution.py:149
  223.7 19.3 %all-gather.2 = f32[16,1,256]{2,1,0:T(1,128)S(1)} all-gather(f32[1,1,256]{2,1,0:T(1,128)S(1)} %get-tuple-element.18), channel_id=1, replica_groups=mesh['z'=16,'h'=2,'l'=2,'x'=4,'c'=2] {'l','x','c'}, dimensions={0}, use_global_device_ids=true | all-gather | bytes 17408 | tf_op jit(solution)/shard_map/all_gather | solution.py:143
  246.7 43.4 %all-gather.7 = f16[4352,256]{1,0:T(8,128)(2,1)S(1)} all-gather(f16[272,256]{1,0:T(8,128)(2,1)S(1)} %concatenate.11), channel_id=3, replica_groups=mesh['z'=16,'h'=2,'l'=2,'x'=4,'c'=2] {'z'}, dimensions={0}, use_global_device_ids=true | all-gather | bytes 2367488 | tf_op jit(solution)/shard_map/all_gather | solution.py:160
  (44 shorter events, 12.5 us)
Async XLA Ops:
  8.9 10.5 %collective-permute-start = (bf16[128,512]{1,0:T(8,128)(2,1)S(1)}, bf16[128,512]{1,0:T(8,128)(2,1)S(1)}, u32[]{:S(2)}, u32[]{:S(2)}) collective-permute-start(bf16[128,512]{1,0:T(8,128)(2,1)S(1)} %constant_dynamic-update-slice_fusion), channel_id=1, source_target_pairs={{0,16},{16,0},{1,17},{17,1},{2,18},{18,2},{3,19},{19,3},{4,20},{20... | collective-permute-start | bytes 393224 | tf_op jit(solution)/shard_map/ppermute | solution.py:20
  22.5 51.7 %all-to-all-start = ((bf16[8,2,512,256]{3,2,1,0:T(8,128)(2,1)}), bf16[8,2,512,256]{3,2,1,0:T(8,128)(2,1)}, u32[]{:S(2)}, u32[]{:S(2)}) async-start(bf16[8,2,512,256]{3,2,1,0:T(8,128)(2,1)} %broadcast_in_dim.8), calls=%async_computation | async-start | bytes 8388608 | tf_op jit(solution)/shard_map/all_to_all | solution.py:123
  27.1 85.3 %all-gather.6.cloned.1.call-start = ((), (), s32[]{:S(2)}) async-start(), calls=%async_computation.4 | async-start | bytes 4456448 | tf_op jit(solution)/shard_map/all_gather | solution.py:122
  27.8 187.1 %reduce-scatter.2.cloned.1.call-start = ((), (), s32[]{:S(2)}) async-start(), calls=%async_computation.3 | async-start | bytes 2228224 | tf_op jit(solution)/shard_map/reduce_scatter | solution.py:135
  74.3 9.4 %collective-permute-start.1 = (bf16[8,2,512,256]{3,2,1,0:T(8,128)(2,1)}, bf16[8,2,512,256]{3,2,1,0:T(8,128)(2,1)}, u32[]{:S(2)}, u32[]{:S(2)}) collective-permute-start(bf16[8,2,512,256]{3,2,1,0:T(8,128)(2,1)} %all-to-all-done.own), channel_id=1, source_target_pairs={{0,1},{1,0},{2,3},{3,2},{4,5},{5,4},{6,7},{7,6},{8,9},{9,8},{10,11... | collective-permute-start | bytes 12582920 | tf_op jit(solution)/shard_map/ppermute | solution.py:20
  112.3 2.2 copy-start
  122.7 23.5 %copy-start.3 = (s32[2]{0:T(128)S(1)}, s32[2]{0:T(128)}, u32[]{:S(2)}) copy-start(s32[2]{0:T(128)} %param.13) | copy-start | bytes 28
  122.7 23.5 %copy-start.2 = (f32[1,2,256]{2,1,0:T(2,128)S(1)}, f32[1,2,256]{2,1,0:T(2,128)}, u32[]{:S(2)}) copy-start(f32[1,2,256]{2,1,0:T(2,128)} %param.12) | copy-start | bytes 6148
  122.7 16.1 %collective-permute-start.2 = (bf16[512,256]{1,0:T(8,128)(2,1)S(1)}, bf16[512,256]{1,0:T(8,128)(2,1)S(1)}, u32[]{:S(2)}, u32[]{:S(2)}) collective-permute-start(bf16[512,256]{1,0:T(8,128)(2,1)S(1)} %get-tuple-element.9.refs_0_), channel_id=1, source_target_pairs={{0,8},{8,0},{1,9},{9,1},{2,10},{10,2},{3,11},{11,3},{4,12},{12,4},... | collective-permute-start | bytes 786440 | tf_op jit(solution)/shard_map/ppermute | solution.py:20
  126.1 15.3 %collective-permute-start.5 = (bf16[512,256]{1,0:T(8,128)(2,1)S(1)}, bf16[512,256]{1,0:T(8,128)(2,1)S(1)}, u32[]{:S(2)}, u32[]{:S(2)}) collective-permute-start(bf16[512,256]{1,0:T(8,128)(2,1)S(1)} %get-tuple-element.10.refs_4_), channel_id=1, source_target_pairs={{0,2},{2,4},{4,6},{6,0},{1,3},{3,5},{5,7},{7,1},{8,10},{10,12},{12... | collective-permute-start | bytes 786440 | tf_op jit(solution)/shard_map/ppermute | solution.py:25
  129.3 12.0 %collective-permute-start.6 = (bf16[512,256]{1,0:T(8,128)(2,1)S(1)}, bf16[512,256]{1,0:T(8,128)(2,1)S(1)}, u32[]{:S(2)}, u32[]{:S(2)}) collective-permute-start(bf16[512,256]{1,0:T(8,128)(2,1)S(1)} %get-tuple-element.10.refs_4_), channel_id=1, source_target_pairs={{0,6},{2,0},{4,2},{6,4},{1,7},{3,1},{5,3},{7,5},{8,14},{10,8},{12,... | collective-permute-start | bytes 786440 | tf_op jit(solution)/shard_map/ppermute | solution.py:25
  133.1 9.8 %collective-permute-start.7 = (bf16[512,256]{1,0:T(8,128)(2,1)S(1)}, bf16[512,256]{1,0:T(8,128)(2,1)S(1)}, u32[]{:S(2)}, u32[]{:S(2)}) collective-permute-start(bf16[512,256]{1,0:T(8,128)(2,1)S(1)} %get-tuple-element.10.refs_4_), channel_id=1, source_target_pairs={{0,4},{2,6},{4,0},{6,2},{1,5},{3,7},{5,1},{7,3},{8,12},{10,14},{12... | collective-permute-start | bytes 786440 | tf_op jit(solution)/shard_map/ppermute | solution.py:25
  136.8 6.1 %collective-permute-start.3 = (bf16[512,256]{1,0:T(8,128)(2,1)S(1)}, bf16[512,256]{1,0:T(8,128)(2,1)S(1)}, u32[]{:S(2)}, u32[]{:S(2)}) collective-permute-start(bf16[512,256]{1,0:T(8,128)(2,1)S(1)} %get-tuple-element.9.refs_0_), channel_id=1, source_target_pairs={{0,1},{1,0},{2,3},{3,2},{4,5},{5,4},{6,7},{7,6},{8,9},{9,8},{10,11... | collective-permute-start | bytes 786440 | tf_op jit(solution)/shard_map/ppermute | solution.py:20
  138.8 4.1 %collective-permute-start.4 = (bf16[512,256]{1,0:T(8,128)(2,1)S(1)}, bf16[512,256]{1,0:T(8,128)(2,1)S(1)}, u32[]{:S(2)}, u32[]{:S(2)}) collective-permute-start(bf16[512,256]{1,0:T(8,128)(2,1)S(1)} %collective-permute-done.2.refs_1_), channel_id=1, source_target_pairs={{0,1},{1,0},{2,3},{3,2},{4,5},{5,4},{6,7},{7,6},{8,9},{9,8},{10,11... | collective-permute-start | bytes 786440 | tf_op jit(solution)/shard_map/ppermute | solution.py:20
  175.9 7.0 %collective-permute-start.8 = (f32[2,256]{1,0:T(2,128)S(1)}, f32[2,256]{1,0:T(2,128)S(1)}, u32[]{:S(2)}, u32[]{:S(2)}) collective-permute-start(f32[2,256]{1,0:T(2,128)S(1)} %psum.7), channel_id=1, source_target_pairs={{0,16},{16,0},{1,17},{17,1},{2,18},{18,2},{3,19},{19,3},{4,20},{20... | collective-permute-start | bytes 6152 | tf_op jit(solution)/shard_map/ppermute | solution.py:20
  182.9 108.3 %copy-start.1 = (f32[2,256]{1,0:T(2,128)}, f32[2,256]{1,0:T(2,128)S(1)}, u32[]{:S(2)}) copy-start(f32[2,256]{1,0:T(2,128)S(1)} %add.90) | copy-start | bytes 6148
  216.5 27.9 %all-to-all-start.1 = ((bf16[8,64,256]{2,1,0:T(8,128)(2,1)}), bf16[8,64,256]{2,1,0:T(8,128)(2,1)S(1)}, u32[]{:S(2)}, u32[]{:S(2)}) async-start(bf16[8,64,256]{2,1,0:T(8,128)(2,1)} %bitcast.13), calls=%async_computation.2 | async-start | bytes 524288 | tf_op jit(solution)/shard_map/all_to_all | solution.py:149
Sparse Core Ops, SparseCore 0:
  30.6 81.7 all-gather.5
  146.2 68.6 reduce-scatter.1

commit v2 on v1

v2 whole, which is shorter than its diff:
```python
import functools
import math

import jax
import jax.numpy as jnp
from jax import lax
from jax.experimental import pallas as pl
from jax.experimental.pallas import tpu as pltpu
from jax.sharding import Mesh, PartitionSpec as P

EMA_WEIGHT = 0.5
DAMPING = 0.01
Z = ("z1", "z0")
DP = ("z1", "z0", "h")
MP = ("l", "x", "c")
BF16 = jnp.bfloat16
F32 = jnp.float32


def swap(array, axis):
    return lax.ppermute(array, axis, [(0, 1), (1, 0)])


def project_kernel(limit, inputs, basis, proj_out, stat_out, total, *, masked):
    step = pl.program_id(0)

    @pl.when(step == 0)
    def _():
        total[...] = jnp.zeros_like(total)

    depth, width = inputs.shape[-1], basis.shape[-1]
    total[...] += sum(
        jnp.dot(inputs[i, 0], basis[i].reshape(depth, width), preferred_element_type=F32) for i in range(inputs.shape[0])
    )

    @pl.when(step == pl.num_programs(0) - 1)
    def _():
        rounded = total[...].astype(BF16)
        valid = lax.broadcasted_iota(jnp.int32, total.shape, 0) < limit[0]
        kept = jnp.where(valid, rounded.astype(F32), 0.0)
        stat_out[...] = jnp.sum(kept * kept, axis=0, keepdims=True)
        for i in range(proj_out.shape[0]):
            proj_out[i] = kept.astype(BF16) if masked else rounded


def project(limit, inputs, side, basis, masked, copies):
    parts, _, tokens, depth = inputs.shape
    width = basis.shape[-1]
    group = 4
    return pl.pallas_call(
        functools.partial(project_kernel, masked=masked),
        grid_spec=pltpu.PrefetchScalarGridSpec(
            num_scalar_prefetch=1,
            grid=(parts // group,),
            in_specs=[
                pl.BlockSpec((group, 1, tokens, depth), lambda k, s: (k, side, 0, 0)),
                pl.BlockSpec((group, 2, depth // 2, width), lambda k, s: (k, 0, 0, 0)),
            ],
            out_specs=[
                pl.BlockSpec((copies, tokens, width), lambda k, s: (0, 0, 0)),
                pl.BlockSpec((1, width), lambda k, s: (0, 0)),
            ],
            scratch_shapes=[pltpu.VMEM((tokens, width), F32)],
        ),
        out_shape=[
            jax.ShapeDtypeStruct((copies, tokens, width), BF16),
            jax.ShapeDtypeStruct((1, width), F32),
        ],
        compiler_params=pltpu.CompilerParams(vmem_limit_bytes=60 << 20),
        cost_estimate=pl.CostEstimate(flops=2 * parts * tokens * depth * width, bytes_accessed=7 << 20, transcendentals=0),
    )(limit, inputs, basis)


def pack(values):
    values = values.astype(F32)
    parts, rows, width = values.shape
    top = jnp.max(jnp.abs(values), axis=1)
    power = jnp.where(top > 0, jnp.clip(jnp.floor(14.0 - jnp.log2(top)), -100.0, 126.0), 0.0)
    scaled = (values * jnp.exp2(power)[:, None]).astype(jnp.float16).reshape(parts * rows, width)
    return jnp.concatenate([scaled, jnp.pad(power.astype(jnp.float16), ((0, 8 - parts), (0, 0)))], axis=0)


def unpack(packed, parts):
    rows = packed.shape[-2] - 8
    part = rows // parts

    def one(i):
        back = jnp.exp2(-packed[..., rows + i : rows + i + 1, :].astype(F32))
        return (packed[..., i * part : (i + 1) * part, :].astype(F32) * back).astype(BF16)

    return [one(i) for i in range(parts)]


def term_kernel(places, *refs):
    grads, acts, out = refs[:4], refs[4], refs[5]
    rows, width = out.shape[3:]
    parts = width // rows
    for g in range(4):
        first = places[g] * (parts // 2)
        for a in range(4):
            tile = lax.dot_general(grads[g][0], acts[a], (((0,), (0,)), ((), ())), preferred_element_type=F32)
            tile = tile.astype(BF16).reshape(parts, rows, width)
            for p in range(parts):
                out[first + p // 2, p % 2, a] = tile[p]


def term(places, grads, acts, chunks):
    _, tokens, width = acts.shape
    whole = pl.BlockSpec(memory_space=pltpu.VMEM)
    return pl.pallas_call(
        term_kernel,
        in_specs=[pl.BlockSpec(memory_space=pltpu.SMEM)] + [whole] * 5,
        out_specs=whole,
        out_shape=jax.ShapeDtypeStruct((chunks // 2, 2, 4, 4 * width // chunks, width), BF16),
        compiler_params=pltpu.CompilerParams(vmem_limit_bytes=32 << 20),
        cost_estimate=pl.CostEstimate(flops=32 * tokens * width * width, bytes_accessed=4 << 20, transcendentals=0),
    )(places, *grads, acts)


def local(activations, out_grads, valid_len, basis_act, basis_grad, eig_state, owner_table):
    z, h, l, x, c = (lax.axis_index(a) for a in (Z, "h", "l", "x", "c"))
    chunks = lax.axis_size(Z)
    tokens, width = activations.shape
    token_total = tokens * chunks * lax.axis_size("h")

    bases = pack(jnp.stack([basis_act, basis_grad]))
    activations, out_grads, bases = lax.optimization_barrier((activations, out_grads, bases))
    paired = swap(bases, "h")
    all_inputs = lax.all_gather(jnp.stack([activations, out_grads]), MP, axis=0)
    bases = jnp.stack([jnp.where(h == 0, bases, paired), jnp.where(h == 0, paired, bases)])
    bases = lax.all_gather(bases, Z, axis=0)
    whole_act, whole_grad = unpack(bases, 2)

    act, stat_act = project(valid_len, all_inputs, 0, whole_act, True, 4)
    acts = lax.all_to_all(act, "x", 0, 0)
    grad, stat_grad = project(valid_len, all_inputs, 1, whole_grad, False, 1)
    far = swap(grad, "l")
    grads = [grad, far, swap(grad, "c"), swap(far, "c")]
    q = 2 * l + c
    places = jnp.stack([q, q ^ 2, q ^ 1, q ^ 3]).astype(jnp.int32)
    partial_term = term(places, grads, acts, chunks)
    stat = jnp.concatenate([stat_act, stat_grad], axis=0)
    partial_term, stat = lax.optimization_barrier((partial_term, stat))
    summed = lax.psum_scatter(partial_term, "z1", scatter_dimension=0, tiled=True)[0]

    rank = z * 2 + h
    mine = (owner_table == rank).astype(F32)
    part = (1.0 - EMA_WEIGHT) * (stat / token_total) + EMA_WEIGHT * mine[:, None] * eig_state[0]
    part = lax.psum(part, Z)
    eigen = part + swap(part, "h")
    new_state = eigen[None]
    eigen_rows = lax.all_gather(eigen[1], MP, axis=0).reshape(2, 4, 2, width)
    eigen_rows = lax.dynamic_index_in_dim(eigen_rows, z >> 3, 0, keepdims=False)
    eigen_rows = lax.dynamic_index_in_dim(eigen_rows, (z >> 2) & 1, 1, keepdims=False)
    rows = partial_term.shape[3]
    eigen_rows = lax.dynamic_slice_in_dim(eigen_rows, (z & 3) * rows, rows, axis=1)

    summed, eigen_rows = lax.optimization_barrier((summed, eigen_rows))
    moved = jnp.broadcast_to(summed[:, None], (2, 2, 4, rows, width)).reshape(16, rows, width)
    moved = lax.all_to_all(moved, ("z0", "h", "x"), 0, 0).reshape(4, 4, rows, width).astype(F32)
    denom = eigen_rows[:, :, None] * eigen[0][None, None, :] + DAMPING
    values = jnp.sum(moved, axis=0) / math.sqrt(token_total) / denom
    (full,) = unpack(lax.all_gather(pack(values.reshape(1, 4 * rows, width)), Z, axis=0), 1)
    full = full.reshape(2, 2, 4, 4, rows, width).transpose(0, 3, 1, 2, 4, 5)
    return (full.reshape(chunks * 4 * rows, width), new_state)


def solution(mesh):
    fine = Mesh(mesh.devices.reshape(8, 2, 2, 2, 4, 2), ("z1", "z0", "h", "l", "x", "c"))
    placed = (P(DP, MP), P(DP, MP), P(DP), P(DP, MP), P(DP, MP), P(DP, None, MP), P())
    return jax.shard_map(
        local, mesh=fine, in_specs=placed, out_specs=(P(None, MP), P(DP, None, MP)), check_vma=False
    )
```

time: 300 us -> 258 us (0.86)
  the two profiles are of different devices: /device:TPU:16 before, /device:TPU:2 now
where the time goes in v2:
time: 258 us; the launch traced here: 257 us
  blocking collectives  161 us (62%)
  starting transfers between devices  29.6 us (11%)
  waiting for transfers between devices  24.9 us (10%)
  between operations  14.9 us (6%)
  Pallas kernels  13.7 us (5%)
  other arithmetic  9 us (3%)
  local copies, waits for them, and re-layouts  4.46 us (2%)
    all_gather x1, blocking collectives, local(): bases = lax.all_gather(bases, Z, axis=0)  69 us
    all_gather x1, blocking collectives, local(): lax.all_gather(pack(values.reshape(1, 4 * rows, width)), Z, axis=0)  44.4 us
    psum x1, blocking collectives, local(): part = lax.psum(part, Z)  30.3 us
    ppermute x5, starting transfers between devices, swap(): return lax.ppermute(array, axis, [(0, 1), (1, 0)])  18.1 us
    all_gather x1, blocking collectives, local(): eigen_rows = lax.all_gather(eigen[1], MP, axis=0).reshape(2, 4, 2, width)  17.1 us
    pallas_call x2, Pallas kernels, project(): pl.pallas_call(functools.partial(project_kernel, masked=masked), grid_spe...  10.6 us
    all_to_all x1, waiting for transfers between devices, local(): lax.all_to_all(moved, ('z0', 'h', 'x'), 0, 0).reshape(4, 4, rows, width)  9.84 us
    ppermute x5, waiting for transfers between devices, swap(): return lax.ppermute(array, axis, [(0, 1), (1, 0)])  8.27 us
  transfers between devices with their start and end apart: 9, of which 6 were waited for; matrix products, arithmetic and copies ran while one was open for 2% of the time, Pallas kernels for 2%

profile of v2, /device:TPU:2, one launch (start us, length us, event | category | flops | bytes accessed | tf_op | source)
XLA Modules:
  0.0 257.4 jit_solution(11365573590353289634)
XLA Ops:
  9.1 1.9 pad_maximum_fusion
  11.0 5.1 %collective-permute-start = (f16[264,256]{1,0:T(8,128)(2,1)S(1)}, f16[264,256]{1,0:T(8,128)(2,1)S(1)}, u32[]{:S(2)}, u32[]{:S(2)}) collective-permute-start(f16[264,256]{1,0:T(8,128)(2,1)S(1)} %fusion.6), channel_id=1, source_target_pairs={{0,16},{16,0},{1,17},{17,1},{2,18},{18,2},{3,19},{19,3},{4,20},{20... | collective-permute-start | bytes 405512 | tf_op jit(solution)/shard_map/ppermute | solution.py:21
  16.8 3.0 %collective-permute-done = f16[264,256]{1,0:T(8,128)(2,1)S(1)} collective-permute-done((f16[264,256]{1,0:T(8,128)(2,1)S(1)}, f16[264,256]{1,0:T(8,128)(2,1)S(1)}, u32[]{:S(2)}, u32[]{:S(2)}) %collective-permute-start) | collective-permute-done | bytes 135200 | tf_op jit(solution)/shard_map/ppermute | solution.py:21
  19.9 69.0 %all-gather.9 = f16[32,264,256]{2,1,0:T(8,128)(2,1)S(1)} all-gather(f16[2,264,256]{2,1,0:T(8,128)(2,1)S(1)} %pad_maximum_fusion.1), channel_id=3, replica_groups=mesh['z1'=8,'z0'=2,'h'=2,'l'=2,'x'=4,'c'=2] {'z1','z0'}, dimensions={0}, use_global_device_ids=true | all-gather | bytes 4595712 | tf_op jit(solution)/shard_map/all_gather | solution.py:131
  89.0 3.3 %multiply_convert_fusion.1 = (bf16[16,2,128,256]{3,2,1,0:T(8,128)(2,1)}, bf16[16,2,128,256]{3,2,1,0:T(8,128)(2,1)}) fusion(f16[16,2,264,256]{3,2,1,0:T(8,128)(2,1)S(1)} %bitcast.48, f32[16,2,256]{2,1,0:T(2,128)S(1)} %get-tuple-element.38, f32[16,2,256]{2,1,0:T(2,128)S(1)} %get-tuple-element.39), kind=kLoop, calls=%fused_computation.1 | loop fusion | flops 6291456 | bytes 8454144 | tf_op jit(solution)/shard_map/convert_element_type | solution.py:89
  92.3 5.5 %shard_map.87 = (bf16[4,512,256]{2,1,0:T(8,128)(2,1)}, f32[1,256]{1,0:T(1,128)}) custom-call(s32[1]{0:T(128)S(6)} %copy.23.limit, bf16[16,2,512,256]{3,2,1,0:T(8,128)(2,1)} %bitcast.45, bf16[16,2,128,256]{3,2,1,0:T(8,128)(2,1)} %get-tuple-element.24.basis), custom_call_target="tpu_custom_call" | custom-call | flops 1073741824 | bytes 7340032 | tf_op jit(solution)/shard_map/pallas_call | solution.py:50
  97.8 4.8 %all-to-all-start = ((bf16[4,512,256]{2,1,0:T(8,128)(2,1)}), bf16[4,512,256]{2,1,0:T(8,128)(2,1)S(1)}, u32[]{:S(2)}, u32[]{:S(2)}) async-start(bf16[4,512,256]{2,1,0:T(8,128)(2,1)} %get-tuple-element.17), calls=%async_computation | async-start | bytes 2097152 | tf_op jit(solution)/shard_map/all_to_all | solution.py:135
  102.6 5.1 %shard_map.86 = (bf16[1,512,256]{2,1,0:T(8,128)(2,1)}, f32[1,256]{1,0:T(1,128)}) custom-call(s32[1]{0:T(128)S(6)} %copy.23.limit, bf16[16,2,512,256]{3,2,1,0:T(8,128)(2,1)} %bitcast.46, bf16[16,2,128,256]{3,2,1,0:T(8,128)(2,1)} %get-tuple-element.25.basis), custom_call_target="tpu_custom_call" | custom-call | flops 1073741824 | bytes 7340032 | tf_op jit(solution)/shard_map/pallas_call | solution.py:50
  107.7 3.6 %collective-permute-start.1 = (bf16[1,512,256]{2,1,0:T(8,128)(2,1)}, bf16[1,512,256]{2,1,0:T(8,128)(2,1)S(1)}, u32[]{:S(2)}, u32[]{:S(2)}) collective-permute-start(bf16[1,512,256]{2,1,0:T(8,128)(2,1)} %get-tuple-element.16.refs_0_), channel_id=1, source_target_pairs={{0,8},{8,0},{1,9},{9,1},{2,10},{10,2},{3,11},{11,3},{4,12},{12,4},... | collective-permute-start | bytes 786440 | tf_op jit(solution)/shard_map/ppermute | solution.py:21
  111.3 1.9 collective-permute-start.2
  113.2 3.1 %collective-permute-done.1.refs_1_ = bf16[1,512,256]{2,1,0:T(8,128)(2,1)S(1)} collective-permute-done((bf16[1,512,256]{2,1,0:T(8,128)(2,1)}, bf16[1,512,256]{2,1,0:T(8,128)(2,1)S(1)}, u32[]{:S(2)}, u32[]{:S(2)}) %collective-permute-start.1) | collective-permute-done | bytes 262176 | tf_op jit(solution)/shard_map/ppermute | solution.py:21
  116.3 1.9 collective-permute-start.3
  119.7 0.9 copy-done
  120.7 3.2 %shard_map.88 = bf16[8,2,4,64,256]{4,3,2,1,0:T(8,128)(2,1)} custom-call(s32[4]{0:T(128)S(1)} %pad_add_fusion.places, bf16[1,512,256]{2,1,0:T(8,128)(2,1)S(1)} %copy-done, bf16[1,512,256]{2,1,0:T(8,128)(2,1)S(1)} %collective-permute-done.1.refs_1_, bf16[1,512,256]{2,1,0:T(8,128)(2,1)S(1)} %collective-permute-done.2.refs_2_, ...), custom_call_target="tpu_custom_call" | custom-call | flops 1073741824 | bytes 4194304 | tf_op jit(solution)/shard_map/pallas_call | solution.py:110
  124.0 30.3 %psum.7 = f32[2,256]{1,0:T(2,128)S(1)} all-reduce(f32[2,256]{1,0:T(2,128)S(1)} %fusion.14), channel_id=1, replica_groups=mesh['z1'=8,'z0'=2,'h'=2,'l'=2,'x'=4,'c'=2] {'z1','z0'}, use_global_device_ids=true, to_apply=%region_2.3 | all-reduce | flops 512 | bytes 4096 | tf_op jit(solution)/shard_map/psum | solution.py:149
  154.3 5.5 %collective-permute-start.4 = (f32[2,256]{1,0:T(2,128)S(1)}, f32[2,256]{1,0:T(2,128)S(1)}, u32[]{:S(2)}, u32[]{:S(2)}) collective-permute-start(f32[2,256]{1,0:T(2,128)S(1)} %psum.7), channel_id=1, source_target_pairs={{0,16},{16,0},{1,17},{17,1},{2,18},{18,2},{3,19},{19,3},{4,20},{20... | collective-permute-start | bytes 6152 | tf_op jit(solution)/shard_map/ppermute | solution.py:21
  159.8 1.5 collective-permute-done.4
  161.4 17.1 %all-gather.3 = f32[16,1,256]{2,1,0:T(1,128)S(1)} all-gather(f32[1,1,256]{2,1,0:T(1,128)S(1)} %get-tuple-element.32), channel_id=1, replica_groups=mesh['z1'=8,'z0'=2,'h'=2,'l'=2,'x'=4,'c'=2] {'l','x','c'}, dimensions={0}, use_global_device_ids=true | all-gather | bytes 17408 | tf_op jit(solution)/shard_map/all_gather | solution.py:152
  178.6 6.8 %reduce-scatter.2.cloned.1.call-done = bf16[1,2,4,64,256]{4,3,2,1,0:T(8,128)(2,1)} async-done(((bf16[8,2,4,64,256]{4,3,2,1,0:T(8,128)(2,1)}), bf16[1,2,4,64,256]{4,3,2,1,0:T(8,128)(2,1)}) %reduce-scatter.2.cloned.1.call-update) | async-done | bytes 262160 | tf_op jit(solution)/shard_map/reduce_scatter | solution.py:144
  185.4 1.8 broadcast_in_dim.7
  187.2 6.7 %all-to-all-start.1 = ((bf16[16,64,256]{2,1,0:T(8,128)(2,1)}), bf16[16,64,256]{2,1,0:T(8,128)(2,1)S(1)}, u32[]{:S(2)}, u32[]{:S(2)}) async-start(bf16[16,64,256]{2,1,0:T(8,128)(2,1)} %bitcast.17), calls=%async_computation.2 | async-start | bytes 1048576 | tf_op jit(solution)/shard_map/all_to_all | solution.py:160
  193.9 9.8 %all-to-all-done.1 = bf16[16,64,256]{2,1,0:T(8,128)(2,1)S(1)} async-done(((bf16[16,64,256]{2,1,0:T(8,128)(2,1)}), bf16[16,64,256]{2,1,0:T(8,128)(2,1)S(1)}, u32[]{:S(2)}, u32[]{:S(2)}) %all-to-all-start.1) | async-done | bytes 524320 | tf_op jit(solution)/shard_map/all_to_all | solution.py:160
  204.2 44.4 %all-gather.10 = f16[4224,256]{1,0:T(8,128)(2,1)S(1)} all-gather(f16[264,256]{1,0:T(8,128)(2,1)S(1)} %fusion.7), channel_id=4, replica_groups=mesh['z1'=8,'z0'=2,'h'=2,'l'=2,'x'=4,'c'=2] {'z1','z0'}, dimensions={0}, use_global_device_ids=true | all-gather | bytes 2297856 | tf_op jit(solution)/shard_map/all_gather | solution.py:163
  249.1 1.5 copy.15
  (44 shorter events, 4.9 us)
Async XLA Ops:
  7.2 85.1 %all-gather.8.cloned.1.call-start = ((), (), s32[]{:S(2)}) async-start(), calls=%async_computation.4 | async-start | bytes 8912896 | tf_op jit(solution)/shard_map/all_gather | solution.py:129
  11.0 8.7 %collective-permute-start = (f16[264,256]{1,0:T(8,128)(2,1)S(1)}, f16[264,256]{1,0:T(8,128)(2,1)S(1)}, u32[]{:S(2)}, u32[]{:S(2)}) collective-permute-start(f16[264,256]{1,0:T(8,128)(2,1)S(1)} %fusion.6), channel_id=1, source_target_pairs={{0,16},{16,0},{1,17},{17,1},{2,18},{18,2},{3,19},{19,3},{4,20},{20... | collective-permute-start | bytes 405512 | tf_op jit(solution)/shard_map/ppermute | solution.py:21
  97.8 21.9 %all-to-all-start = ((bf16[4,512,256]{2,1,0:T(8,128)(2,1)}), bf16[4,512,256]{2,1,0:T(8,128)(2,1)S(1)}, u32[]{:S(2)}, u32[]{:S(2)}) async-start(bf16[4,512,256]{2,1,0:T(8,128)(2,1)} %get-tuple-element.17), calls=%async_computation | async-start | bytes 2097152 | tf_op jit(solution)/shard_map/all_to_all | solution.py:135
  102.6 82.8 %reduce-scatter.2.cloned.1.call-start = ((), (), s32[]{:S(2)}) async-start(), calls=%async_computation.3 | async-start | bytes 2359296 | tf_op jit(solution)/shard_map/reduce_scatter | solution.py:144
  102.6 15.7 %copy-start.3 = (f32[1,256]{1,0:T(1,128)S(1)}, f32[1,256]{1,0:T(1,128)}, u32[]{:S(2)}) copy-start(f32[1,256]{1,0:T(1,128)} %get-tuple-element.18) | copy-start | bytes 3076
  107.7 16.2 %copy-start.4 = (s32[2]{0:T(128)S(1)}, s32[2]{0:T(128)}, u32[]{:S(2)}) copy-start(s32[2]{0:T(128)} %param.13) | copy-start | bytes 28
  107.7 16.2 %copy-start.2 = (f32[1,2,256]{2,1,0:T(2,128)S(1)}, f32[1,2,256]{2,1,0:T(2,128)}, u32[]{:S(2)}) copy-start(f32[1,2,256]{2,1,0:T(2,128)} %param.12) | copy-start | bytes 6148
  107.7 8.6 %collective-permute-start.1 = (bf16[1,512,256]{2,1,0:T(8,128)(2,1)}, bf16[1,512,256]{2,1,0:T(8,128)(2,1)S(1)}, u32[]{:S(2)}, u32[]{:S(2)}) collective-permute-start(bf16[1,512,256]{2,1,0:T(8,128)(2,1)} %get-tuple-element.16.refs_0_), channel_id=1, source_target_pairs={{0,8},{8,0},{1,9},{9,1},{2,10},{10,2},{3,11},{11,3},{4,12},{12,4},... | collective-permute-start | bytes 786440 | tf_op jit(solution)/shard_map/ppermute | solution.py:21
  111.3 7.7 %collective-permute-start.2 = (bf16[1,512,256]{2,1,0:T(8,128)(2,1)}, bf16[1,512,256]{2,1,0:T(8,128)(2,1)S(1)}, u32[]{:S(2)}, u32[]{:S(2)}) collective-permute-start(bf16[1,512,256]{2,1,0:T(8,128)(2,1)} %get-tuple-element.16.refs_0_), channel_id=1, source_target_pairs={{0,1},{1,0},{2,3},{3,2},{4,5},{5,4},{6,7},{7,6},{8,9},{9,8},{10,11... | collective-permute-start | bytes 786440 | tf_op jit(solution)/shard_map/ppermute | solution.py:21
  116.3 3.4 %collective-permute-start.3 = (bf16[1,512,256]{2,1,0:T(8,128)(2,1)S(1)}, bf16[1,512,256]{2,1,0:T(8,128)(2,1)S(1)}, u32[]{:S(2)}, u32[]{:S(2)}) collective-permute-start(bf16[1,512,256]{2,1,0:T(8,128)(2,1)S(1)} %collective-permute-done.1.refs_1_), channel_id=1, source_target_pairs={{0,1},{1,0},{2,3},{3,2},{4,5},{5,4},{6,7},{7,6},{8,9},{9,8},{10,11... | collective-permute-start | bytes 786440 | tf_op jit(solution)/shard_map/ppermute | solution.py:21
  119.7 1.0 copy-start
  154.3 7.1 %collective-permute-start.4 = (f32[2,256]{1,0:T(2,128)S(1)}, f32[2,256]{1,0:T(2,128)S(1)}, u32[]{:S(2)}, u32[]{:S(2)}) collective-permute-start(f32[2,256]{1,0:T(2,128)S(1)} %psum.7), channel_id=1, source_target_pairs={{0,16},{16,0},{1,17},{17,1},{2,18},{18,2},{3,19},{19,3},{4,20},{20... | collective-permute-start | bytes 6152 | tf_op jit(solution)/shard_map/ppermute | solution.py:21
  161.4 87.8 %copy-start.1 = (f32[2,256]{1,0:T(2,128)}, f32[2,256]{1,0:T(2,128)S(1)}, u32[]{:S(2)}) copy-start(f32[2,256]{1,0:T(2,128)S(1)} %add.62) | copy-start | bytes 6148
  187.2 16.6 %all-to-all-start.1 = ((bf16[16,64,256]{2,1,0:T(8,128)(2,1)}), bf16[16,64,256]{2,1,0:T(8,128)(2,1)S(1)}, u32[]{:S(2)}, u32[]{:S(2)}) async-start(bf16[16,64,256]{2,1,0:T(8,128)(2,1)} %bitcast.17), calls=%async_computation.2 | async-start | bytes 1048576 | tf_op jit(solution)/shard_map/all_to_all | solution.py:160
Sparse Core Ops, SparseCore 0:
  11.1 64.1 all-gather.7
  124.0 61.3 reduce-scatter.1

commit v3 on v2

--- a/solution.py
+++ b/solution.py
@@ -46,7 +46,7 @@
 def project(limit, inputs, side, basis, masked, copies):
     parts, _, tokens, depth = inputs.shape
     width = basis.shape[-1]
-    group = 4
+    group = 8
     return pl.pallas_call(
         functools.partial(project_kernel, masked=masked),
         grid_spec=pltpu.PrefetchScalarGridSpec(
@@ -66,7 +66,7 @@
             jax.ShapeDtypeStruct((copies, tokens, width), BF16),
             jax.ShapeDtypeStruct((1, width), F32),
         ],
-        compiler_params=pltpu.CompilerParams(vmem_limit_bytes=60 << 20),
+        compiler_params=pltpu.CompilerParams(vmem_limit_bytes=48 << 20),
         cost_estimate=pl.CostEstimate(flops=2 * parts * tokens * depth * width, bytes_accessed=7 << 20, transcendentals=0),
     )(limit, inputs, basis)
 
@@ -127,8 +127,8 @@
     activations, out_grads, bases = lax.optimization_barrier((activations, out_grads, bases))
     paired = swap(bases, "h")
     all_inputs = lax.all_gather(jnp.stack([activations, out_grads]), MP, axis=0)
-    bases = jnp.stack([jnp.where(h == 0, bases, paired), jnp.where(h == 0, paired, bases)])
-    bases = lax.all_gather(bases, Z, axis=0)
+    bases = jnp.concatenate([jnp.where(h == 0, bases, paired), jnp.where(h == 0, paired, bases)], axis=0)
+    bases = lax.all_gather(bases, Z, axis=0).reshape(chunks, 2, *paired.shape)
     whole_act, whole_grad = unpack(bases, 2)
 
     act, stat_act = project(valid_len, all_inputs, 0, whole_act, True, 4)
@@ -141,7 +141,9 @@
     partial_term = term(places, grads, acts, chunks)
     stat = jnp.concatenate([stat_act, stat_grad], axis=0)
     partial_term, stat = lax.optimization_barrier((partial_term, stat))
-    summed = lax.psum_scatter(partial_term, "z1", scatter_dimension=0, tiled=True)[0]
+    rows = partial_term.shape[3]
+    summed = lax.psum_scatter(partial_term.reshape(-1, width), "z1", scatter_dimension=0, tiled=True)
+    summed = summed.reshape(2, 4, rows, width)
 
     rank = z * 2 + h
     mine = (owner_table == rank).astype(F32)
@@ -149,10 +151,9 @@
     part = lax.psum(part, Z)
     eigen = part + swap(part, "h")
     new_state = eigen[None]
-    eigen_rows = lax.all_gather(eigen[1], MP, axis=0).reshape(2, 4, 2, width)
+    eigen_rows = lax.all_to_all(jnp.broadcast_to(eigen[1], (16, 1, width)), MP, 0, 0).reshape(2, 4, 2, width)
     eigen_rows = lax.dynamic_index_in_dim(eigen_rows, z >> 3, 0, keepdims=False)
     eigen_rows = lax.dynamic_index_in_dim(eigen_rows, (z >> 2) & 1, 1, keepdims=False)
-    rows = partial_term.shape[3]
     eigen_rows = lax.dynamic_slice_in_dim(eigen_rows, (z & 3) * rows, rows, axis=1)
 
     summed, eigen_rows = lax.optimization_barrier((summed, eigen_rows))

time: 258 us -> 254 us (0.984)
  blocking collectives: 161 us -> 142 us
  waiting for transfers between devices: 24.9 us -> 35.3 us
  starting transfers between devices: 29.6 us -> 36.4 us
  Pallas kernels: 13.7 us -> 9.71 us
    all_gather x2 -> x1, blocking collectives: 86.1 us -> 69 us  [local(): bases = lax.all_gather(bases, Z, axis=0).reshape(chunks, 2, *paired.shape)]
    all_to_all x0 -> x1, starting transfers between devices: none -> 5.98 us  [local(): lax.all_to_all(jnp.broadcast_to(eigen[1], (16, 1, width)), MP, 0, 0)]
    reduce_scatter x1, waiting for transfers between devices: 6.77 us -> 12 us  [local(): lax.psum_scatter(partial_term.reshape(-1, width), 'z1', scatter_dimension...]
    all_to_all x0 -> x1, waiting for transfers between devices: none -> 4.72 us  [local(): lax.all_to_all(jnp.broadcast_to(eigen[1], (16, 1, width)), MP, 0, 0)]
    pallas_call x2, Pallas kernels: 10.6 us -> 6.54 us  [project(): pl.pallas_call(functools.partial(project_kernel, masked=masked), grid_spe...]
  transfers between devices with their start and end apart: 9 -> 10, of which waited for: 6 -> 7; matrix products, arithmetic and copies ran while one was open for 2% -> 2% of each run, Pallas kernels for 2% -> 1%
where the time goes in v3:
time: 254 us; the launch traced here: 253 us
  blocking collectives  142 us (56%)
  starting transfers between devices  36.4 us (14%)
  waiting for transfers between devices  35.3 us (14%)
  between operations  14.9 us (6%)
  Pallas kernels  9.71 us (4%)
  other arithmetic  7.6 us (3%)
  local copies, waits for them, and re-layouts  6.68 us (3%)
    all_gather x1, blocking collectives, local(): bases = lax.all_gather(bases, Z, axis=0).reshape(chunks, 2, *paired.shape)  69 us
    all_gather x1, blocking collectives, local(): lax.all_gather(pack(values.reshape(1, 4 * rows, width)), Z, axis=0)  43.1 us
    psum x1, blocking collectives, local(): part = lax.psum(part, Z)  30.3 us
    ppermute x5, starting transfers between devices, swap(): return lax.ppermute(array, axis, [(0, 1), (1, 0)])  17.9 us
    reduce_scatter x1, waiting for transfers between devices, local(): lax.psum_scatter(partial_term.reshape(-1, width), 'z1', scatter_dimension...  12 us
    all_to_all x1, waiting for transfers between devices, local(): lax.all_to_all(moved, ('z0', 'h', 'x'), 0, 0).reshape(4, 4, rows, width)  9.84 us
    ppermute x5, waiting for transfers between devices, swap(): return lax.ppermute(array, axis, [(0, 1), (1, 0)])  8.75 us
    all_to_all x1, starting transfers between devices, local(): lax.all_to_all(moved, ('z0', 'h', 'x'), 0, 0).reshape(4, 4, rows, width)  7.63 us
  transfers between devices with their start and end apart: 10, of which 7 were waited for; matrix products, arithmetic and copies ran while one was open for 2% of the time, Pallas kernels for 1%

profile of v3, /device:TPU:2, one launch (start us, length us, event | category | flops | bytes accessed | tf_op | source)
XLA Modules:
  0.0 253.0 jit_solution(5777746161731564669)
XLA Ops:
  9.1 1.9 pad_maximum_fusion
  11.0 5.1 %collective-permute-start = (f16[264,256]{1,0:T(8,128)(2,1)S(1)}, f16[264,256]{1,0:T(8,128)(2,1)S(1)}, u32[]{:S(2)}, u32[]{:S(2)}) collective-permute-start(f16[264,256]{1,0:T(8,128)(2,1)S(1)} %fusion.6), channel_id=1, source_target_pairs={{0,16},{16,0},{1,17},{17,1},{2,18},{18,2},{3,19},{19,3},{4,20},{20... | collective-permute-start | bytes 405512 | tf_op jit(solution)/shard_map/ppermute | solution.py:21
  16.8 3.0 %collective-permute-done = f16[264,256]{1,0:T(8,128)(2,1)S(1)} collective-permute-done((f16[264,256]{1,0:T(8,128)(2,1)S(1)}, f16[264,256]{1,0:T(8,128)(2,1)S(1)}, u32[]{:S(2)}, u32[]{:S(2)}) %collective-permute-start) | collective-permute-done | bytes 135200 | tf_op jit(solution)/shard_map/ppermute | solution.py:21
  19.9 69.0 %all-gather.8 = f16[8448,256]{1,0:T(8,128)(2,1)S(1)} all-gather(f16[528,256]{1,0:T(8,128)(2,1)S(1)} %pad_maximum_fusion.1), channel_id=3, replica_groups=mesh['z1'=8,'z0'=2,'h'=2,'l'=2,'x'=4,'c'=2] {'z1','z0'}, dimensions={0}, use_global_device_ids=true | all-gather | bytes 4595712 | tf_op jit(solution)/shard_map/all_gather | solution.py:131
  89.0 2.5 %multiply_convert_fusion.1 = (bf16[16,2,128,256]{3,2,1,0:T(8,128)(2,1)}, bf16[16,2,128,256]{3,2,1,0:T(8,128)(2,1)S(1)}) fusion(f16[16,2,264,256]{3,2,1,0:T(8,128)(2,1)S(1)} %bitcast.44, f32[16,2,256]{2,1,0:T(2,128)S(1)} %get-tuple-element.38, f32[16,2,256]{2,1,0:T(2,128)S(1)} %get-tuple-element.39), kind=kLoop, calls=%fused_computation.1 | loop fusion | flops 6291456 | bytes 8454144 | tf_op jit(solution)/shard_map/convert_element_type | solution.py:89
  91.6 1.6 copy-done
  93.2 3.3 %shard_map.87 = (bf16[4,512,256]{2,1,0:T(8,128)(2,1)S(1)}, f32[1,256]{1,0:T(1,128)S(1)}) custom-call(s32[1]{0:T(128)S(6)} %copy.23.limit, bf16[16,2,512,256]{3,2,1,0:T(8,128)(2,1)} %bitcast.41, bf16[16,2,128,256]{3,2,1,0:T(8,128)(2,1)S(1)} %copy-done), custom_call_target="tpu_custom_call" | custom-call | flops 1073741824 | bytes 7340032 | tf_op jit(solution)/shard_map/pallas_call | solution.py:50
  97.4 4.8 %all-to-all-start = ((bf16[4,512,256]{2,1,0:T(8,128)(2,1)}), bf16[4,512,256]{2,1,0:T(8,128)(2,1)S(1)}, u32[]{:S(2)}, u32[]{:S(2)}) async-start(bf16[4,512,256]{2,1,0:T(8,128)(2,1)} %copy-done.1), calls=%async_computation | async-start | bytes 2097152 | tf_op jit(solution)/shard_map/all_to_all | solution.py:135
  102.3 3.2 %shard_map.86 = (bf16[1,512,256]{2,1,0:T(8,128)(2,1)S(1)}, f32[1,256]{1,0:T(1,128)S(1)}) custom-call(s32[1]{0:T(128)S(6)} %copy.23.limit, bf16[16,2,512,256]{3,2,1,0:T(8,128)(2,1)} %bitcast.42, bf16[16,2,128,256]{3,2,1,0:T(8,128)(2,1)S(1)} %get-tuple-element.25.basis), custom_call_target="tpu_custom_call" | custom-call | flops 1073741824 | bytes 7340032 | tf_op jit(solution)/shard_map/pallas_call | solution.py:50
  105.5 3.5 %collective-permute-start.1 = (bf16[1,512,256]{2,1,0:T(8,128)(2,1)S(1)}, bf16[1,512,256]{2,1,0:T(8,128)(2,1)S(1)}, u32[]{:S(2)}, u32[]{:S(2)}) collective-permute-start(bf16[1,512,256]{2,1,0:T(8,128)(2,1)S(1)} %get-tuple-element.16.refs_0_), channel_id=1, source_target_pairs={{0,8},{8,0},{1,9},{9,1},{2,10},{10,2},{3,11},{11,3},{4,12},{12,4},... | collective-permute-start | bytes 786440 | tf_op jit(solution)/shard_map/ppermute | solution.py:21
  109.0 1.9 collective-permute-start.2
  111.0 2.8 %collective-permute-done.1.refs_1_ = bf16[1,512,256]{2,1,0:T(8,128)(2,1)S(1)} collective-permute-done((bf16[1,512,256]{2,1,0:T(8,128)(2,1)S(1)}, bf16[1,512,256]{2,1,0:T(8,128)(2,1)S(1)}, u32[]{:S(2)}, u32[]{:S(2)}) %collective-permute-start.1) | collective-permute-done | bytes 262176 | tf_op jit(solution)/shard_map/ppermute | solution.py:21
  113.8 1.9 collective-permute-start.3
  117.2 3.2 %shard_map.88 = bf16[8,2,4,64,256]{4,3,2,1,0:T(8,128)(2,1)} custom-call(s32[4]{0:T(128)S(1)} %pad_add_fusion.places, bf16[1,512,256]{2,1,0:T(8,128)(2,1)S(1)} %get-tuple-element.16.refs_0_, bf16[1,512,256]{2,1,0:T(8,128)(2,1)S(1)} %collective-permute-done.1.refs_1_, bf16[1,512,256]{2,1,0:T(8,128)(2,1)S(1)} %collective-permute-done.2.refs_2_, ...), custom_call_target="tpu_custom_call" | custom-call | flops 1073741824 | bytes 4194304 | tf_op jit(solution)/shard_map/pallas_call | solution.py:110
  120.5 30.3 %psum.7 = f32[2,256]{1,0:T(2,128)S(1)} all-reduce(f32[2,256]{1,0:T(2,128)S(1)} %fusion.14), channel_id=1, replica_groups=mesh['z1'=8,'z0'=2,'h'=2,'l'=2,'x'=4,'c'=2] {'z1','z0'}, use_global_device_ids=true, to_apply=%region_2.3 | all-reduce | flops 512 | bytes 4096 | tf_op jit(solution)/shard_map/psum | solution.py:151
  150.9 5.5 %collective-permute-start.4 = (f32[2,256]{1,0:T(2,128)S(1)}, f32[2,256]{1,0:T(2,128)S(1)}, u32[]{:S(2)}, u32[]{:S(2)}) collective-permute-start(f32[2,256]{1,0:T(2,128)S(1)} %psum.7), channel_id=1, source_target_pairs={{0,16},{16,0},{1,17},{17,1},{2,18},{18,2},{3,19},{19,3},{4,20},{20... | collective-permute-start | bytes 6152 | tf_op jit(solution)/shard_map/ppermute | solution.py:21
  156.4 1.5 collective-permute-done.4
  158.5 6.0 %all-to-all-start.1 = ((f32[16,1,256]{2,1,0:T(1,128)}), f32[16,1,256]{2,1,0:T(1,128)S(1)}, u32[]{:S(2)}, u32[]{:S(2)}) async-start(f32[16,1,256]{2,1,0:T(1,128)} %broadcast_in_dim.9), calls=%async_computation.2 | async-start | bytes 32768 | tf_op jit(solution)/shard_map/all_to_all | solution.py:154
  164.5 4.7 %all-to-all-done.1 = f32[16,1,256]{2,1,0:T(1,128)S(1)} async-done(((f32[16,1,256]{2,1,0:T(1,128)}), f32[16,1,256]{2,1,0:T(1,128)S(1)}, u32[]{:S(2)}, u32[]{:S(2)}) %all-to-all-start.1) | async-done | bytes 16416 | tf_op jit(solution)/shard_map/all_to_all | solution.py:154
  169.4 12.0 %reduce-scatter.2.cloned.1.call-done = bf16[512,256]{1,0:T(8,128)(2,1)} async-done(((bf16[4096,256]{1,0:T(8,128)(2,1)}), bf16[512,256]{1,0:T(8,128)(2,1)}) %reduce-scatter.2.cloned.1.call-update) | async-done | bytes 262160 | tf_op jit(solution)/shard_map/reduce_scatter | solution.py:145
  181.4 1.8 broadcast_in_dim.10
  183.2 7.6 %all-to-all-start.2 = ((bf16[16,64,256]{2,1,0:T(8,128)(2,1)}), bf16[16,64,256]{2,1,0:T(8,128)(2,1)S(1)}, u32[]{:S(2)}, u32[]{:S(2)}) async-start(bf16[16,64,256]{2,1,0:T(8,128)(2,1)} %bitcast.16), calls=%async_computation.3 | async-start | bytes 1048576 | tf_op jit(solution)/shard_map/all_to_all | solution.py:161
  190.9 9.8 %all-to-all-done.2 = bf16[16,64,256]{2,1,0:T(8,128)(2,1)S(1)} async-done(((bf16[16,64,256]{2,1,0:T(8,128)(2,1)}), bf16[16,64,256]{2,1,0:T(8,128)(2,1)S(1)}, u32[]{:S(2)}, u32[]{:S(2)}) %all-to-all-start.2) | async-done | bytes 524320 | tf_op jit(solution)/shard_map/all_to_all | solution.py:161
  201.1 43.1 %all-gather.9 = f16[4224,256]{1,0:T(8,128)(2,1)S(1)} all-gather(f16[264,256]{1,0:T(8,128)(2,1)S(1)} %fusion.7), channel_id=4, replica_groups=mesh['z1'=8,'z0'=2,'h'=2,'l'=2,'x'=4,'c'=2] {'z1','z0'}, dimensions={0}, use_global_device_ids=true | all-gather | bytes 2297856 | tf_op jit(solution)/shard_map/all_gather | solution.py:164
  (46 shorter events, 7.9 us)
Async XLA Ops:
  7.2 84.4 %all-gather.7.cloned.1.call-start = ((), (), s32[]{:S(2)}) async-start(), calls=%async_computation.5 | async-start | bytes 8912896 | tf_op jit(solution)/shard_map/all_gather | solution.py:129
  11.0 8.7 %collective-permute-start = (f16[264,256]{1,0:T(8,128)(2,1)S(1)}, f16[264,256]{1,0:T(8,128)(2,1)S(1)}, u32[]{:S(2)}, u32[]{:S(2)}) collective-permute-start(f16[264,256]{1,0:T(8,128)(2,1)S(1)} %fusion.6), channel_id=1, source_target_pairs={{0,16},{16,0},{1,17},{17,1},{2,18},{18,2},{3,19},{19,3},{4,20},{20... | collective-permute-start | bytes 405512 | tf_op jit(solution)/shard_map/ppermute | solution.py:21
  91.6 1.6 copy-start
  96.5 1.0 copy-start.1
  97.4 19.8 %all-to-all-start = ((bf16[4,512,256]{2,1,0:T(8,128)(2,1)}), bf16[4,512,256]{2,1,0:T(8,128)(2,1)S(1)}, u32[]{:S(2)}, u32[]{:S(2)}) async-start(bf16[4,512,256]{2,1,0:T(8,128)(2,1)} %copy-done.1), calls=%async_computation | async-start | bytes 2097152 | tf_op jit(solution)/shard_map/all_to_all | solution.py:135
  102.3 79.1 %reduce-scatter.2.cloned.1.call-start = ((), (), s32[]{:S(2)}) async-start(), calls=%async_computation.4 | async-start | bytes 2359296 | tf_op jit(solution)/shard_map/reduce_scatter | solution.py:145
  105.5 14.9 %copy-start.4 = (s32[2]{0:T(128)S(1)}, s32[2]{0:T(128)}, u32[]{:S(2)}) copy-start(s32[2]{0:T(128)} %param.13) | copy-start | bytes 28
  105.5 14.9 %copy-start.3 = (f32[1,2,256]{2,1,0:T(2,128)S(1)}, f32[1,2,256]{2,1,0:T(2,128)}, u32[]{:S(2)}) copy-start(f32[1,2,256]{2,1,0:T(2,128)} %param.12) | copy-start | bytes 6148
  105.5 8.3 %collective-permute-start.1 = (bf16[1,512,256]{2,1,0:T(8,128)(2,1)S(1)}, bf16[1,512,256]{2,1,0:T(8,128)(2,1)S(1)}, u32[]{:S(2)}, u32[]{:S(2)}) collective-permute-start(bf16[1,512,256]{2,1,0:T(8,128)(2,1)S(1)} %get-tuple-element.16.refs_0_), channel_id=1, source_target_pairs={{0,8},{8,0},{1,9},{9,1},{2,10},{10,2},{3,11},{11,3},{4,12},{12,4},... | collective-permute-start | bytes 786440 | tf_op jit(solution)/shard_map/ppermute | solution.py:21
  109.0 6.8 %collective-permute-start.2 = (bf16[1,512,256]{2,1,0:T(8,128)(2,1)S(1)}, bf16[1,512,256]{2,1,0:T(8,128)(2,1)S(1)}, u32[]{:S(2)}, u32[]{:S(2)}) collective-permute-start(bf16[1,512,256]{2,1,0:T(8,128)(2,1)S(1)} %get-tuple-element.16.refs_0_), channel_id=1, source_target_pairs={{0,1},{1,0},{2,3},{3,2},{4,5},{5,4},{6,7},{7,6},{8,9},{9,8},{10,11... | collective-permute-start | bytes 786440 | tf_op jit(solution)/shard_map/ppermute | solution.py:21
  113.8 3.4 %collective-permute-start.3 = (bf16[1,512,256]{2,1,0:T(8,128)(2,1)S(1)}, bf16[1,512,256]{2,1,0:T(8,128)(2,1)S(1)}, u32[]{:S(2)}, u32[]{:S(2)}) collective-permute-start(bf16[1,512,256]{2,1,0:T(8,128)(2,1)S(1)} %collective-permute-done.1.refs_1_), channel_id=1, source_target_pairs={{0,1},{1,0},{2,3},{3,2},{4,5},{5,4},{6,7},{7,6},{8,9},{9,8},{10,11... | collective-permute-start | bytes 786440 | tf_op jit(solution)/shard_map/ppermute | solution.py:21
  150.9 7.1 %collective-permute-start.4 = (f32[2,256]{1,0:T(2,128)S(1)}, f32[2,256]{1,0:T(2,128)S(1)}, u32[]{:S(2)}, u32[]{:S(2)}) collective-permute-start(f32[2,256]{1,0:T(2,128)S(1)} %psum.7), channel_id=1, source_target_pairs={{0,16},{16,0},{1,17},{17,1},{2,18},{18,2},{3,19},{19,3},{4,20},{20... | collective-permute-start | bytes 6152 | tf_op jit(solution)/shard_map/ppermute | solution.py:21
  157.9 86.8 %copy-start.2 = (f32[2,256]{1,0:T(2,128)}, f32[2,256]{1,0:T(2,128)S(1)}, u32[]{:S(2)}) copy-start(f32[2,256]{1,0:T(2,128)S(1)} %add.62) | copy-start | bytes 6148
  158.5 10.7 %all-to-all-start.1 = ((f32[16,1,256]{2,1,0:T(1,128)}), f32[16,1,256]{2,1,0:T(1,128)S(1)}, u32[]{:S(2)}, u32[]{:S(2)}) async-start(f32[16,1,256]{2,1,0:T(1,128)} %broadcast_in_dim.9), calls=%async_computation.2 | async-start | bytes 32768 | tf_op jit(solution)/shard_map/all_to_all | solution.py:154
  183.2 17.6 %all-to-all-start.2 = ((bf16[16,64,256]{2,1,0:T(8,128)(2,1)}), bf16[16,64,256]{2,1,0:T(8,128)(2,1)S(1)}, u32[]{:S(2)}, u32[]{:S(2)}) async-start(bf16[16,64,256]{2,1,0:T(8,128)(2,1)} %bitcast.16), calls=%async_computation.3 | async-start | bytes 1048576 | tf_op jit(solution)/shard_map/all_to_all | solution.py:161
Sparse Core Ops, SparseCore 0:
  11.1 64.1 all-gather.6
  120.5 60.7 reduce-scatter.1

commit v4 on v3

--- a/solution.py
+++ b/solution.py
@@ -66,7 +66,7 @@
             jax.ShapeDtypeStruct((copies, tokens, width), BF16),
             jax.ShapeDtypeStruct((1, width), F32),
         ],
-        compiler_params=pltpu.CompilerParams(vmem_limit_bytes=48 << 20),
+        compiler_params=pltpu.CompilerParams(vmem_limit_bytes=44 << 20),
         cost_estimate=pl.CostEstimate(flops=2 * parts * tokens * depth * width, bytes_accessed=7 << 20, transcendentals=0),
     )(limit, inputs, basis)
 

time: 254 us -> 254 us (level)
  no operation moved by 1% of the time
where the time goes in v4:
time: 254 us; the launch traced here: 253 us
  blocking collectives  142 us (56%)
  starting transfers between devices  36.4 us (14%)
  waiting for transfers between devices  35.3 us (14%)
  between operations  14.9 us (6%)
  Pallas kernels  9.71 us (4%)
  other arithmetic  7.6 us (3%)
  local copies, waits for them, and re-layouts  6.68 us (3%)
    all_gather x1, blocking collectives, local(): bases = lax.all_gather(bases, Z, axis=0).reshape(chunks, 2, *paired.shape)  69 us
    all_gather x1, blocking collectives, local(): lax.all_gather(pack(values.reshape(1, 4 * rows, width)), Z, axis=0)  43.1 us
    psum x1, blocking collectives, local(): part = lax.psum(part, Z)  30.3 us
    ppermute x5, starting transfers between devices, swap(): return lax.ppermute(array, axis, [(0, 1), (1, 0)])  17.9 us
    reduce_scatter x1, waiting for transfers between devices, local(): lax.psum_scatter(partial_term.reshape(-1, width), 'z1', scatter_dimension...  12 us
    all_to_all x1, waiting for transfers between devices, local(): lax.all_to_all(moved, ('z0', 'h', 'x'), 0, 0).reshape(4, 4, rows, width)  9.84 us
    ppermute x5, waiting for transfers between devices, swap(): return lax.ppermute(array, axis, [(0, 1), (1, 0)])  8.75 us
    all_to_all x1, starting transfers between devices, local(): lax.all_to_all(moved, ('z0', 'h', 'x'), 0, 0).reshape(4, 4, rows, width)  7.63 us
  transfers between devices with their start and end apart: 10, of which 7 were waited for; matrix products, arithmetic and copies ran while one was open for 2% of the time, Pallas kernels for 1%

profile of v4, /device:TPU:2, one launch (start us, length us, event | category | flops | bytes accessed | tf_op | source)
XLA Modules:
  0.0 253.0 jit_solution(10323855057155207734)
XLA Ops:
  9.1 1.9 pad_maximum_fusion
  11.0 5.1 %collective-permute-start = (f16[264,256]{1,0:T(8,128)(2,1)S(1)}, f16[264,256]{1,0:T(8,128)(2,1)S(1)}, u32[]{:S(2)}, u32[]{:S(2)}) collective-permute-start(f16[264,256]{1,0:T(8,128)(2,1)S(1)} %fusion.6), channel_id=1, source_target_pairs={{0,16},{16,0},{1,17},{17,1},{2,18},{18,2},{3,19},{19,3},{4,20},{20... | collective-permute-start | bytes 405512 | tf_op jit(solution)/shard_map/ppermute | solution.py:21
  16.8 3.0 %collective-permute-done = f16[264,256]{1,0:T(8,128)(2,1)S(1)} collective-permute-done((f16[264,256]{1,0:T(8,128)(2,1)S(1)}, f16[264,256]{1,0:T(8,128)(2,1)S(1)}, u32[]{:S(2)}, u32[]{:S(2)}) %collective-permute-start) | collective-permute-done | bytes 135200 | tf_op jit(solution)/shard_map/ppermute | solution.py:21
  19.9 69.0 %all-gather.8 = f16[8448,256]{1,0:T(8,128)(2,1)S(1)} all-gather(f16[528,256]{1,0:T(8,128)(2,1)S(1)} %pad_maximum_fusion.1), channel_id=3, replica_groups=mesh['z1'=8,'z0'=2,'h'=2,'l'=2,'x'=4,'c'=2] {'z1','z0'}, dimensions={0}, use_global_device_ids=true | all-gather | bytes 4595712 | tf_op jit(solution)/shard_map/all_gather | solution.py:131
  89.0 2.5 %multiply_convert_fusion.1 = (bf16[16,2,128,256]{3,2,1,0:T(8,128)(2,1)}, bf16[16,2,128,256]{3,2,1,0:T(8,128)(2,1)S(1)}) fusion(f16[16,2,264,256]{3,2,1,0:T(8,128)(2,1)S(1)} %bitcast.44, f32[16,2,256]{2,1,0:T(2,128)S(1)} %get-tuple-element.38, f32[16,2,256]{2,1,0:T(2,128)S(1)} %get-tuple-element.39), kind=kLoop, calls=%fused_computation.1 | loop fusion | flops 6291456 | bytes 8454144 | tf_op jit(solution)/shard_map/convert_element_type | solution.py:89
  91.6 1.6 copy-done
  93.2 3.3 %shard_map.87 = (bf16[4,512,256]{2,1,0:T(8,128)(2,1)S(1)}, f32[1,256]{1,0:T(1,128)S(1)}) custom-call(s32[1]{0:T(128)S(6)} %copy.23.limit, bf16[16,2,512,256]{3,2,1,0:T(8,128)(2,1)} %bitcast.41, bf16[16,2,128,256]{3,2,1,0:T(8,128)(2,1)S(1)} %copy-done), custom_call_target="tpu_custom_call" | custom-call | flops 1073741824 | bytes 7340032 | tf_op jit(solution)/shard_map/pallas_call | solution.py:50
  97.4 4.8 %all-to-all-start = ((bf16[4,512,256]{2,1,0:T(8,128)(2,1)}), bf16[4,512,256]{2,1,0:T(8,128)(2,1)S(1)}, u32[]{:S(2)}, u32[]{:S(2)}) async-start(bf16[4,512,256]{2,1,0:T(8,128)(2,1)} %copy-done.1), calls=%async_computation | async-start | bytes 2097152 | tf_op jit(solution)/shard_map/all_to_all | solution.py:135
  102.3 3.2 %shard_map.86 = (bf16[1,512,256]{2,1,0:T(8,128)(2,1)S(1)}, f32[1,256]{1,0:T(1,128)S(1)}) custom-call(s32[1]{0:T(128)S(6)} %copy.23.limit, bf16[16,2,512,256]{3,2,1,0:T(8,128)(2,1)} %bitcast.42, bf16[16,2,128,256]{3,2,1,0:T(8,128)(2,1)S(1)} %get-tuple-element.25.basis), custom_call_target="tpu_custom_call" | custom-call | flops 1073741824 | bytes 7340032 | tf_op jit(solution)/shard_map/pallas_call | solution.py:50
  105.5 3.5 %collective-permute-start.1 = (bf16[1,512,256]{2,1,0:T(8,128)(2,1)S(1)}, bf16[1,512,256]{2,1,0:T(8,128)(2,1)S(1)}, u32[]{:S(2)}, u32[]{:S(2)}) collective-permute-start(bf16[1,512,256]{2,1,0:T(8,128)(2,1)S(1)} %get-tuple-element.16.refs_0_), channel_id=1, source_target_pairs={{0,8},{8,0},{1,9},{9,1},{2,10},{10,2},{3,11},{11,3},{4,12},{12,4},... | collective-permute-start | bytes 786440 | tf_op jit(solution)/shard_map/ppermute | solution.py:21
  109.0 1.9 collective-permute-start.2
  111.0 2.8 %collective-permute-done.1.refs_1_ = bf16[1,512,256]{2,1,0:T(8,128)(2,1)S(1)} collective-permute-done((bf16[1,512,256]{2,1,0:T(8,128)(2,1)S(1)}, bf16[1,512,256]{2,1,0:T(8,128)(2,1)S(1)}, u32[]{:S(2)}, u32[]{:S(2)}) %collective-permute-start.1) | collective-permute-done | bytes 262176 | tf_op jit(solution)/shard_map/ppermute | solution.py:21
  113.8 1.9 collective-permute-start.3
  117.2 3.2 %shard_map.88 = bf16[8,2,4,64,256]{4,3,2,1,0:T(8,128)(2,1)} custom-call(s32[4]{0:T(128)S(1)} %pad_add_fusion.places, bf16[1,512,256]{2,1,0:T(8,128)(2,1)S(1)} %get-tuple-element.16.refs_0_, bf16[1,512,256]{2,1,0:T(8,128)(2,1)S(1)} %collective-permute-done.1.refs_1_, bf16[1,512,256]{2,1,0:T(8,128)(2,1)S(1)} %collective-permute-done.2.refs_2_, ...), custom_call_target="tpu_custom_call" | custom-call | flops 1073741824 | bytes 4194304 | tf_op jit(solution)/shard_map/pallas_call | solution.py:110
  120.5 30.3 %psum.7 = f32[2,256]{1,0:T(2,128)S(1)} all-reduce(f32[2,256]{1,0:T(2,128)S(1)} %fusion.14), channel_id=1, replica_groups=mesh['z1'=8,'z0'=2,'h'=2,'l'=2,'x'=4,'c'=2] {'z1','z0'}, use_global_device_ids=true, to_apply=%region_2.3 | all-reduce | flops 512 | bytes 4096 | tf_op jit(solution)/shard_map/psum | solution.py:151
  150.9 5.5 %collective-permute-start.4 = (f32[2,256]{1,0:T(2,128)S(1)}, f32[2,256]{1,0:T(2,128)S(1)}, u32[]{:S(2)}, u32[]{:S(2)}) collective-permute-start(f32[2,256]{1,0:T(2,128)S(1)} %psum.7), channel_id=1, source_target_pairs={{0,16},{16,0},{1,17},{17,1},{2,18},{18,2},{3,19},{19,3},{4,20},{20... | collective-permute-start | bytes 6152 | tf_op jit(solution)/shard_map/ppermute | solution.py:21
  156.4 1.5 collective-permute-done.4
  158.5 6.0 %all-to-all-start.1 = ((f32[16,1,256]{2,1,0:T(1,128)}), f32[16,1,256]{2,1,0:T(1,128)S(1)}, u32[]{:S(2)}, u32[]{:S(2)}) async-start(f32[16,1,256]{2,1,0:T(1,128)} %broadcast_in_dim.9), calls=%async_computation.2 | async-start | bytes 32768 | tf_op jit(solution)/shard_map/all_to_all | solution.py:154
  164.5 4.7 %all-to-all-done.1 = f32[16,1,256]{2,1,0:T(1,128)S(1)} async-done(((f32[16,1,256]{2,1,0:T(1,128)}), f32[16,1,256]{2,1,0:T(1,128)S(1)}, u32[]{:S(2)}, u32[]{:S(2)}) %all-to-all-start.1) | async-done | bytes 16416 | tf_op jit(solution)/shard_map/all_to_all | solution.py:154
  169.4 12.0 %reduce-scatter.2.cloned.1.call-done = bf16[512,256]{1,0:T(8,128)(2,1)} async-done(((bf16[4096,256]{1,0:T(8,128)(2,1)}), bf16[512,256]{1,0:T(8,128)(2,1)}) %reduce-scatter.2.cloned.1.call-update) | async-done | bytes 262160 | tf_op jit(solution)/shard_map/reduce_scatter | solution.py:145
  181.4 1.8 broadcast_in_dim.10
  183.2 7.6 %all-to-all-start.2 = ((bf16[16,64,256]{2,1,0:T(8,128)(2,1)}), bf16[16,64,256]{2,1,0:T(8,128)(2,1)S(1)}, u32[]{:S(2)}, u32[]{:S(2)}) async-start(bf16[16,64,256]{2,1,0:T(8,128)(2,1)} %bitcast.16), calls=%async_computation.3 | async-start | bytes 1048576 | tf_op jit(solution)/shard_map/all_to_all | solution.py:161
  190.9 9.8 %all-to-all-done.2 = bf16[16,64,256]{2,1,0:T(8,128)(2,1)S(1)} async-done(((bf16[16,64,256]{2,1,0:T(8,128)(2,1)}), bf16[16,64,256]{2,1,0:T(8,128)(2,1)S(1)}, u32[]{:S(2)}, u32[]{:S(2)}) %all-to-all-start.2) | async-done | bytes 524320 | tf_op jit(solution)/shard_map/all_to_all | solution.py:161
  201.1 43.1 %all-gather.9 = f16[4224,256]{1,0:T(8,128)(2,1)S(1)} all-gather(f16[264,256]{1,0:T(8,128)(2,1)S(1)} %fusion.7), channel_id=4, replica_groups=mesh['z1'=8,'z0'=2,'h'=2,'l'=2,'x'=4,'c'=2] {'z1','z0'}, dimensions={0}, use_global_device_ids=true | all-gather | bytes 2297856 | tf_op jit(solution)/shard_map/all_gather | solution.py:164
  (46 shorter events, 7.9 us)
Async XLA Ops:
  7.2 84.4 %all-gather.7.cloned.1.call-start = ((), (), s32[]{:S(2)}) async-start(), calls=%async_computation.5 | async-start | bytes 8912896 | tf_op jit(solution)/shard_map/all_gather | solution.py:129
  11.0 8.7 %collective-permute-start = (f16[264,256]{1,0:T(8,128)(2,1)S(1)}, f16[264,256]{1,0:T(8,128)(2,1)S(1)}, u32[]{:S(2)}, u32[]{:S(2)}) collective-permute-start(f16[264,256]{1,0:T(8,128)(2,1)S(1)} %fusion.6), channel_id=1, source_target_pairs={{0,16},{16,0},{1,17},{17,1},{2,18},{18,2},{3,19},{19,3},{4,20},{20... | collective-permute-start | bytes 405512 | tf_op jit(solution)/shard_map/ppermute | solution.py:21
  91.6 1.6 copy-start
  96.5 1.0 copy-start.1
  97.4 19.8 %all-to-all-start = ((bf16[4,512,256]{2,1,0:T(8,128)(2,1)}), bf16[4,512,256]{2,1,0:T(8,128)(2,1)S(1)}, u32[]{:S(2)}, u32[]{:S(2)}) async-start(bf16[4,512,256]{2,1,0:T(8,128)(2,1)} %copy-done.1), calls=%async_computation | async-start | bytes 2097152 | tf_op jit(solution)/shard_map/all_to_all | solution.py:135
  102.3 79.1 %reduce-scatter.2.cloned.1.call-start = ((), (), s32[]{:S(2)}) async-start(), calls=%async_computation.4 | async-start | bytes 2359296 | tf_op jit(solution)/shard_map/reduce_scatter | solution.py:145
  105.5 14.9 %copy-start.4 = (s32[2]{0:T(128)S(1)}, s32[2]{0:T(128)}, u32[]{:S(2)}) copy-start(s32[2]{0:T(128)} %param.13) | copy-start | bytes 28
  105.5 14.9 %copy-start.3 = (f32[1,2,256]{2,1,0:T(2,128)S(1)}, f32[1,2,256]{2,1,0:T(2,128)}, u32[]{:S(2)}) copy-start(f32[1,2,256]{2,1,0:T(2,128)} %param.12) | copy-start | bytes 6148
  105.5 8.3 %collective-permute-start.1 = (bf16[1,512,256]{2,1,0:T(8,128)(2,1)S(1)}, bf16[1,512,256]{2,1,0:T(8,128)(2,1)S(1)}, u32[]{:S(2)}, u32[]{:S(2)}) collective-permute-start(bf16[1,512,256]{2,1,0:T(8,128)(2,1)S(1)} %get-tuple-element.16.refs_0_), channel_id=1, source_target_pairs={{0,8},{8,0},{1,9},{9,1},{2,10},{10,2},{3,11},{11,3},{4,12},{12,4},... | collective-permute-start | bytes 786440 | tf_op jit(solution)/shard_map/ppermute | solution.py:21
  109.0 6.8 %collective-permute-start.2 = (bf16[1,512,256]{2,1,0:T(8,128)(2,1)S(1)}, bf16[1,512,256]{2,1,0:T(8,128)(2,1)S(1)}, u32[]{:S(2)}, u32[]{:S(2)}) collective-permute-start(bf16[1,512,256]{2,1,0:T(8,128)(2,1)S(1)} %get-tuple-element.16.refs_0_), channel_id=1, source_target_pairs={{0,1},{1,0},{2,3},{3,2},{4,5},{5,4},{6,7},{7,6},{8,9},{9,8},{10,11... | collective-permute-start | bytes 786440 | tf_op jit(solution)/shard_map/ppermute | solution.py:21
  113.8 3.4 %collective-permute-start.3 = (bf16[1,512,256]{2,1,0:T(8,128)(2,1)S(1)}, bf16[1,512,256]{2,1,0:T(8,128)(2,1)S(1)}, u32[]{:S(2)}, u32[]{:S(2)}) collective-permute-start(bf16[1,512,256]{2,1,0:T(8,128)(2,1)S(1)} %collective-permute-done.1.refs_1_), channel_id=1, source_target_pairs={{0,1},{1,0},{2,3},{3,2},{4,5},{5,4},{6,7},{7,6},{8,9},{9,8},{10,11... | collective-permute-start | bytes 786440 | tf_op jit(solution)/shard_map/ppermute | solution.py:21
  150.9 7.1 %collective-permute-start.4 = (f32[2,256]{1,0:T(2,128)S(1)}, f32[2,256]{1,0:T(2,128)S(1)}, u32[]{:S(2)}, u32[]{:S(2)}) collective-permute-start(f32[2,256]{1,0:T(2,128)S(1)} %psum.7), channel_id=1, source_target_pairs={{0,16},{16,0},{1,17},{17,1},{2,18},{18,2},{3,19},{19,3},{4,20},{20... | collective-permute-start | bytes 6152 | tf_op jit(solution)/shard_map/ppermute | solution.py:21
  157.9 86.8 %copy-start.2 = (f32[2,256]{1,0:T(2,128)}, f32[2,256]{1,0:T(2,128)S(1)}, u32[]{:S(2)}) copy-start(f32[2,256]{1,0:T(2,128)S(1)} %add.62) | copy-start | bytes 6148
  158.5 10.7 %all-to-all-start.1 = ((f32[16,1,256]{2,1,0:T(1,128)}), f32[16,1,256]{2,1,0:T(1,128)S(1)}, u32[]{:S(2)}, u32[]{:S(2)}) async-start(f32[16,1,256]{2,1,0:T(1,128)} %broadcast_in_dim.9), calls=%async_computation.2 | async-start | bytes 32768 | tf_op jit(solution)/shard_map/all_to_all | solution.py:154
  183.2 17.6 %all-to-all-start.2 = ((bf16[16,64,256]{2,1,0:T(8,128)(2,1)}), bf16[16,64,256]{2,1,0:T(8,128)(2,1)S(1)}, u32[]{:S(2)}, u32[]{:S(2)}) async-start(bf16[16,64,256]{2,1,0:T(8,128)(2,1)} %bitcast.16), calls=%async_computation.3 | async-start | bytes 1048576 | tf_op jit(solution)/shard_map/all_to_all | solution.py:161
Sparse Core Ops, SparseCore 0:
  11.1 64.1 all-gather.6
  120.5 60.7 reduce-scatter.1
